TPU v7x, 512 devices: a whole 4x4x16 slice. The times are simulated.
512 devices in a mesh: dp: 32 (over z_lo, x, core), mp: 16 (over z_hi, y).
Axes of the slice: x: 4, y: 4, z: 16 (z_hi: 4, z_lo: 4; z = z_hi * 4 + z_lo), core: 2. Of those that a mesh axis runs over, the one named last changes fastest.
Arguments:
- grads: bfloat16 [32, 2, 256, 28672], P('dp', None, None, 'mp'), may hold values from -6 to 6
- weights: bfloat16 [2, 256, 28672], P(None, 'dp', 'mp'), may hold values from -1.5 to 1.5
- first_moment: float32 [2, 256, 256], P(None, 'dp'), may hold values from -6 to 6
- second_moment: float32 [2, 256, 256], P(None, 'dp'), may hold values from 1 to 16
- old_seeds: int32 [2], replicated, may hold values from 0 to 999999
- new_seeds: int32 [2], replicated, may hold values from 0 to 999999
Outputs:
- new_weights: bfloat16 [2, 256, 28672], P(None, None, 'mp')
- new_first: float32 [2, 256, 256], P(None, 'dp')
- new_second: float32 [2, 256, 256], P(None, 'dp')
Inputs may be any that keep to these rules, and one draw needn't show every extreme that they name: `old_seeds`: seeds of the counter-based generator; old and new seeds are drawn independently. `new_seeds`: seeds of the counter-based generator; old and new seeds are drawn independently.
All inputs are finite; a program needn't handle non-finite values.
Results may differ from a plain program's by a relative error of at most 0.0053.
Values may be sent and summed in bfloat16 or wider, within the bound.
No kernel may reach another device: no remote copies, remote signals or barrier semaphores. Data moves between devices by JAX's collectives and lax.ppermute only.
A program may use at most 64 MiB of HBM per device.

v0:
```python
import math

import jax
import jax.numpy as jnp
from jax import lax
from jax.sharding import PartitionSpec as P


def scramble(values):
    return (values % 46000 * (values // 2 % 46000 + 1) + 12345) % 65521


def generate(seed_value, rank_ids, columns):
    offset = seed_value % 65521
    row_key = (rank_ids * 251 + offset * 3) % 65521
    col_key = scramble((columns * 7 + offset) % 65521)
    hashed = scramble((row_key[:, None] + 2 * col_key[None, :]) % 65521)
    hashed = scramble((hashed * 3 + row_key[:, None]) % 65521)
    spread = math.sqrt(12.0 / rank_ids.shape[0])
    return ((hashed.astype(jnp.float32) + 0.5) / 65521.0 - 0.5) * spread


def inner_rank(left, right):
    return lax.dot_general(
        left, right, (((1,), (1,)), ((), ())), preferred_element_type=jnp.float32
    )


def shards(grads, weights, first_moment, second_moment, old_seeds, new_seeds):
    layers = weights.shape[0]
    rank = first_moment.shape[2]
    ncols = weights.shape[2]
    col_start = lax.axis_index("mp") * ncols
    columns = col_start + jnp.arange(ncols, dtype=jnp.int32)
    rank_ids = jnp.arange(rank, dtype=jnp.int32)
    new_projs = [
        generate(new_seeds[layer_id], rank_ids, columns).astype(jnp.bfloat16)
        for layer_id in range(layers)
    ]
    gathered = []
    firsts = []
    seconds = []
    for layer_id in range(layers):
        new_proj = new_projs[layer_id]
        old_proj = generate(old_seeds[layer_id], rank_ids, columns).astype(jnp.bfloat16)
        gram_matrix = lax.psum(inner_rank(old_proj, new_proj), "mp")
        partial_value = inner_rank(grads[0, layer_id], new_proj)
        owned = lax.psum_scatter(partial_value, "dp", scatter_dimension=0, tiled=True)
        compressed = lax.psum(owned, "mp")
        moment = (
            0.9 * jnp.dot(first_moment[layer_id], gram_matrix, precision=lax.Precision.HIGHEST)
            + 0.1 * compressed
        )
        second = (
            0.95
            * jnp.dot(
                second_moment[layer_id], gram_matrix * gram_matrix, precision=lax.Precision.HIGHEST
            )
            + 0.05 * compressed * compressed
        )
        direction = (moment / (jnp.sqrt(second) + 1e-08)).astype(jnp.bfloat16)
        update = jnp.dot(direction, new_proj, preferred_element_type=jnp.float32)
        block = (weights[layer_id].astype(jnp.float32) - 0.5 * update).astype(jnp.bfloat16)
        gathered.append(lax.all_gather(block, "dp", axis=0, tiled=True))
        firsts.append(moment)
        seconds.append(second)
    new_weights = jnp.stack(gathered)
    return (new_weights, jnp.stack(firsts), jnp.stack(seconds))


def solution(mesh):
    placed = (
        P("dp", None, None, "mp"),
        P(None, "dp", "mp"),
        P(None, "dp", None),
        P(None, "dp", None),
        P(),
        P(),
    )
    return jax.shard_map(
        shards,
        mesh=mesh,
        in_specs=placed,
        out_specs=(P(None, None, "mp"), P(None, "dp", None), P(None, "dp", None)),
        check_vma=False,
    )
```

profile of v0, /device:TPU:1, one launch (start us, length us, event | category | flops | bytes accessed | tf_op | source)
XLA Modules:
  0.0 542.0 jit_solution(2791521066732754462)
XLA Ops:
  8.0 0.0 reduce-scatter.5.cloned.1.call-start
  8.0 1.3 fusion.313
  10.1 11.9 %convolution_bitcast_fusion = f32[256,256]{1,0:T(8,128)} fusion(bf16[1,2,256,1792]{3,2,1,0:T(8,128)(2,1)} %param.6, s32[1792]{0:T(1024)S(1)} %fusion.205, s32[256]{0:T(256)S(1)} %and_select_fusion), kind=kOutput, calls=%fused_computation.211 | convolution fusion | flops 277544960 | bytes 1187840 | tf_op jit(solution)/shard_map/dot_general | solution.py:24
  22.1 0.3 reduce-scatter.3.cloned.1.call-start
  23.1 10.6 %convolution_bitcast_fusion.1 = f32[256,256]{1,0:T(8,128)} fusion(bf16[1,2,256,1792]{3,2,1,0:T(8,128)(2,1)S(1)} %copy-done.3, s32[1792]{0:T(1024)S(1)} %fusion.191, s32[256]{0:T(256)S(1)} %and_select_fusion.2), kind=kOutput, calls=%fused_computation.212 | convolution fusion | flops 277544960 | bytes 1188864 | tf_op jit(solution)/shard_map/dot_general | solution.py:24
  33.8 0.4 all-reduce.4.cloned.1.call-start
  34.2 0.6 fusion.312
  36.1 0.1 fusion.184
  36.2 20.4 %fusion.138 = f32[256,256]{1,0:T(8,128)} fusion(s32[1792]{0:T(1024)S(1)} %fusion.191, s32[256]{0:T(256)S(1)} %and_select_fusion.2, s32[1792]{0:T(1024)S(1)} %get-tuple-element.11, s32[256]{0:T(256)S(1)} %and_select_fusion.3), kind=kOutput, calls=%fused_computation.226 | convolution fusion | flops 320208896 | bytes 278528 | tf_op jit(solution)/shard_map/dot_general | solution.py:24
  56.7 20.8 %fusion.136 = f32[256,256]{1,0:T(8,128)} fusion(s32[1792]{0:T(1024)S(1)} %get-tuple-element.12, s32[256]{0:T(256)S(1)} %and_select_fusion.1, s32[1792]{0:T(1024)S(1)} %fusion.205, s32[256]{0:T(256)S(1)} %and_select_fusion), kind=kOutput, calls=%fused_computation.225 | convolution fusion | flops 320208896 | bytes 278528 | tf_op jit(solution)/shard_map/dot_general | solution.py:24
  77.5 95.8 %reduce-scatter.5.cloned.1.call-done = f32[8,256]{1,0:T(8,128)} async-done(((f32[256,256]{1,0:T(8,128)}), f32[8,256]{1,0:T(8,128)}) %reduce-scatter.5.cloned.1.call-update) | async-done | bytes 8208 | tf_op jit(solution)/shard_map/reduce_scatter | solution.py:48
  173.4 149.7 %reduce-scatter.3.cloned.1.call-done = f32[8,256]{1,0:T(8,128)} async-done(((f32[256,256]{1,0:T(8,128)}), f32[8,256]{1,0:T(8,128)}) %reduce-scatter.3.cloned.1.call-update) | async-done | bytes 8208 | tf_op jit(solution)/shard_map/reduce_scatter | solution.py:48
  323.1 84.7 %all-reduce = (f32[8,256]{1,0:T(8,128)S(1)}, f32[8,256]{1,0:T(8,128)S(1)}) all-reduce(f32[8,256]{1,0:T(8,128)} %reduce-scatter.5.cloned.1.call-done, f32[8,256]{1,0:T(8,128)} %reduce-scatter.3.cloned.1.call-done), channel_id=1, replica_groups=mesh['dp'=32,'mp'=16] {'mp'}, use_global_device_ids=true, to_apply=%region_5.6 | all-reduce | flops 4096 | bytes 32768 | tf_op jit(solution)/shard_map/psum | solution.py:49
  407.8 1.2 fusion.129
  409.0 1.2 fusion.131
  410.1 1.2 fusion.133
  411.4 1.2 fusion.135
  412.6 9.8 %fusion.3 = bf16[8,1792]{1,0:T(8,128)(2,1)S(1)} fusion(s32[1792]{0:T(1024)S(1)} %fusion.205, s32[256]{0:T(256)S(1)} %and_select_fusion, bf16[2,8,1792]{2,1,0:T(8,128)(2,1)S(1)} %copy-done.4, f32[8,256]{1,0:T(8,128)S(1)} %fusion.131, f32[8,256]{1,0:T(8,128)S(1)} %fusion.129), kind=kOutput, calls=%fused_computation.69 | convolution fusion | flops 50067456 | bytes 81920 | tf_op jit(solution)/shard_map/dot_general | solution.py:62
  422.4 57.5 %all_gather.7 = bf16[256,1792]{1,0:T(8,128)(2,1)S(1)} all-gather(bf16[8,1792]{1,0:T(8,128)(2,1)S(1)} %fusion.3), channel_id=1, replica_groups=mesh['dp'=32,'mp'=16] {'dp'}, dimensions={0}, use_global_device_ids=true | all-gather | bytes 946176 | tf_op jit(solution)/shard_map/all_gather | solution.py:64
  479.9 9.8 %fusion.2 = bf16[8,1792]{1,0:T(8,128)(2,1)S(1)} fusion(s32[1792]{0:T(1024)S(1)} %fusion.191, s32[256]{0:T(256)S(1)} %and_select_fusion.2, bf16[2,8,1792]{2,1,0:T(8,128)(2,1)S(1)} %copy-done.4, f32[8,256]{1,0:T(8,128)S(1)} %fusion.135, f32[8,256]{1,0:T(8,128)S(1)} %fusion.133), kind=kOutput, calls=%fused_computation.68 | convolution fusion | flops 50067456 | bytes 81920 | tf_op jit(solution)/shard_map/dot_general | solution.py:62
  489.7 41.9 %all_gather.6 = bf16[256,1792]{1,0:T(8,128)(2,1)S(1)} all-gather(bf16[8,1792]{1,0:T(8,128)(2,1)S(1)} %fusion.2), channel_id=1, replica_groups=mesh['dp'=32,'mp'=16] {'dp'}, dimensions={0}, use_global_device_ids=true | all-gather | bytes 946176 | tf_op jit(solution)/shard_map/all_gather | solution.py:64
  531.6 0.6 pad_maximum_fusion.2
  532.2 0.6 pad_maximum_fusion.1
  532.8 1.4 pad_maximum_fusion
  (20 shorter events, 0.3 us)
Async XLA Ops:
  8.0 165.4 %reduce-scatter.5.cloned.1.call-start = ((), (), s32[]{:S(2)}) async-start(), calls=%async_computation.3 | async-start | bytes 270336 | tf_op jit(solution)/shard_map/reduce_scatter | solution.py:48
  10.1 13.0 %copy-start.3 = (bf16[1,2,256,1792]{3,2,1,0:T(8,128)(2,1)S(1)}, bf16[1,2,256,1792]{3,2,1,0:T(8,128)(2,1)}, u32[]{:S(2)}) copy-start(bf16[1,2,256,1792]{3,2,1,0:T(8,128)(2,1)} %param.6) | copy-start | bytes 5505028
  22.1 301.0 %reduce-scatter.3.cloned.1.call-start = ((), (), s32[]{:S(2)}) async-start(), calls=%async_computation.2 | async-start | bytes 270336 | tf_op jit(solution)/shard_map/reduce_scatter | solution.py:48
  23.1 11.1 %copy-start.2 = (s32[2]{0:T(128)S(1)}, s32[2]{0:T(128)}, u32[]{:S(2)}) copy-start(s32[2]{0:T(128)} %param.10) | copy-start | bytes 28
  33.8 374.0 %all-reduce.4.cloned.1.call-start = ((), (), s32[]{:S(2)}) async-start(), calls=%async_computation.4 | async-start | bytes 1048576 | tf_op jit(solution)/shard_map/psum | solution.py:46
  56.7 351.1 %copy-start = (f32[2,8,256]{2,1,0:T(8,128)S(1)}, f32[2,8,256]{2,1,0:T(8,128)}, u32[]{:S(2)}) copy-start(f32[2,8,256]{2,1,0:T(8,128)} %param.9) | copy-start | bytes 49156
  56.7 352.3 %copy-start.1 = (f32[2,8,256]{2,1,0:T(8,128)S(1)}, f32[2,8,256]{2,1,0:T(8,128)}, u32[]{:S(2)}) copy-start(f32[2,8,256]{2,1,0:T(8,128)} %param.8) | copy-start | bytes 49156
  56.7 355.9 %copy-start.4 = (bf16[2,8,1792]{2,1,0:T(8,128)(2,1)S(1)}, bf16[2,8,1792]{2,1,0:T(8,128)(2,1)}, u32[]{:S(2)}) copy-start(bf16[2,8,1792]{2,1,0:T(8,128)(2,1)} %param.7) | copy-start | bytes 172036
Sparse Core Ops, SparseCore 0:
  22.2 151.1 reduce-scatter.4
  176.1 146.8 reduce-scatter.2
Sparse Core Ops, SparseCore 1:
  77.6 199.6 all-reduce.3
where the time goes:
time: 550 us; the launch traced here: 542 us
  waiting for transfers between devices  246 us (45%)
  blocking collectives  184 us (33%)
  matrix products  88.2 us (16%)
  between operations  18.6 us (3%)
    reduce_scatter x2, waiting for transfers between devices, shards(): lax.psum_scatter(partial_value, 'dp', scatter_dimension=0, tiled=True)  246 us
    all_gather x2, blocking collectives, shards(): gathered.append(lax.all_gather(block, 'dp', axis=0, tiled=True))  99.4 us
    psum x1, blocking collectives, shards(): compressed = lax.psum(owned, 'mp')  84.7 us
    dot_general x4, matrix products, inner_rank(): lax.dot_general(left, right, (((1,), (1,)), ((), ())), preferred_element_...  63.8 us
    dot_general x2, matrix products, shards(): update = jnp.dot(direction, new_proj, preferred_element_type=jnp.float32)  19.6 us
  transfers between devices with their start and end apart: 3, of which 2 were waited for; matrix products, arithmetic and copies ran while one was open for 10% of the time, Pallas kernels for 0%

commit v1 on v0

v1 whole, which is shorter than its diff:
```python
import functools
import math

import jax
import jax.numpy as jnp
from jax import lax
from jax.experimental import pallas as pl
from jax.experimental.pallas import tpu as pltpu
from jax.sharding import PartitionSpec as P

PRIME = 65521
CUT = 46000
F32 = jnp.float32
BF16 = jnp.bfloat16
BOTH = ("dp", "mp")
NT = (((1,), (1,)), ((), ()))
TN = (((0,), (0,)), ((), ()))
HIGHEST = lax.Precision.HIGHEST


def device(z_lo, x, core, z_hi, y):
    return ((z_lo * 4 + x) * 2 + core) * 16 + z_hi * 4 + y


FOUR = range(4)
PLANES = [
    [device(z_lo, x, core, z_hi, y) for x in FOUR for y in FOUR for core in range(2)]
    for z_hi in FOUR
    for z_lo in FOUR
]
LINES = [
    [device(z_lo, x, core, z_hi, y) for z_hi in FOUR for z_lo in FOUR]
    for x in FOUR
    for y in FOUR
    for core in range(2)
]


def below(values, bound):
    return jnp.where(values >= bound, values - bound, values)


def fold(values):
    return values - PRIME * (values >> 16)


def product(values):
    return below(values, CUT) * ((values >> 1) + 1)


def scrambled(values):
    return below(fold(fold(product(values) + 12345)), PRIME)


def row_keys(offset, rank_ids):
    return below(fold(rank_ids * 251 + offset * 3), PRIME)


def column_keys(offset, columns):
    return below(2 * scrambled(below(fold(columns * 7 + offset), PRIME)), PRIME)


def entries(keys, keys_later, columns2, spread):
    first = fold(product(below(keys + columns2, PRIME)))
    second = below(fold(first * 3 + keys_later), PRIME)
    last = fold(product(second) + 12345).astype(F32)
    whole = jnp.floor((last + 0.5) * (1.0 / PRIME))
    return (((last - 32760.0) - whole * float(PRIME)) * (spread / PRIME)).astype(BF16)


def project_kernel(
    place, new_seeds, old_seeds, grads, proj, send, keys, columns2, old_rows, *, rank, cols, spread
):
    layer_id = pl.program_id(0)
    dp, mp = place[0], place[1]
    lanes = lax.broadcasted_iota(jnp.int32, (8, cols), 1) + mp * cols
    row = lax.broadcasted_iota(jnp.int32, (rank, 128), 0)
    tiles = cols // 128
    offset = lax.rem(new_seeds[layer_id], PRIME)
    keys[...] = row_keys(offset, row)
    columns2[...] = column_keys(offset, lanes)

    def wide(narrow):
        return jnp.concatenate([narrow] * tiles, axis=1)

    def both_halves(eight):
        return jnp.concatenate([eight, eight], axis=0)

    def chunk(index, _):
        at = pl.multiple_of(index * 16, 16)
        mine = keys[pl.ds(at, 16), :]
        later = below(mine + 3 * 12345, PRIME)
        for tile in range(tiles):
            cut = slice(tile * 128, tile * 128 + 128)
            proj[0, pl.ds(at, 16), cut] = entries(
                mine, later, both_halves(columns2[:, cut]), spread
            )
        return 0

    lax.fori_loop(0, rank // 16, chunk, 0)
    compressed = lax.dot_general(proj[0], grads[0, 0], NT, preferred_element_type=F32)
    send[:, 0:16, :] = compressed.astype(BF16).reshape(rank // 16, 16, rank)

    mine_layer = dp // (rank // 16)

    @pl.when(layer_id == mine_layer)
    def _():
        old_rows[...] = jnp.zeros_like(old_rows)
        old_offset = lax.rem(old_seeds[layer_id], PRIME)
        at = pl.multiple_of((dp % (rank // 16)) * 16, 16)
        mine = row_keys(old_offset, lax.broadcasted_iota(jnp.int32, (16, 128), 0) + at)
        later = below(mine + 3 * 12345, PRIME)
        columns2[...] = column_keys(old_offset, lanes)
        for tile in range(tiles):
            cut = slice(tile * 128, tile * 128 + 128)
            old_rows[pl.ds(at, 16), cut] = entries(
                mine, later, both_halves(columns2[:, cut]), spread
            )
        gram = lax.dot_general(proj[0], old_rows[...], NT, preferred_element_type=F32)
        send[:, 16:32, :] = gram.astype(BF16).reshape(rank // 16, 16, rank)

    @pl.when(layer_id != mine_layer)
    def _():
        send[:, 16:32, :] = jnp.zeros((rank // 16, 16, rank), BF16)


def sum_kernel(received, send):
    total = received[0].astype(F32)
    for part in range(1, received.shape[0]):
        total = total + received[part].astype(F32)
    send[...] = jnp.broadcast_to(total.astype(BF16)[None], send.shape)


def moment_kernel(place, received, first_moment, second_moment, send):
    z_lo = place[0] // 8
    total = received[0].astype(F32)
    for part in range(1, received.shape[0]):
        total = total + received[part].astype(F32)
    compressed, gram = total[0:16], total[16:32]
    first = (
        0.9
        * lax.dot_general(
            gram, first_moment[0].astype(F32), NT, precision=HIGHEST, preferred_element_type=F32
        )
        + 0.1 * compressed
    )
    second = (
        0.95
        * lax.dot_general(
            gram * gram,
            second_moment[0].astype(F32),
            NT,
            precision=HIGHEST,
            preferred_element_type=F32,
        )
        + 0.05 * compressed * compressed
    )
    direction = (first / (jnp.sqrt(second) + 1e-08)).astype(BF16)
    rows = lax.broadcasted_iota(jnp.int32, (256, 256), 0)
    lanes = lax.broadcasted_iota(jnp.int32, (256, 256), 1)
    picked = jnp.zeros((16, 256), F32)
    for slot, value in enumerate((first, second)):
        high = value.astype(BF16)
        low = (value - high.astype(F32)).astype(BF16)
        for base, part in ((64 * slot, high), (128 + 64 * slot, low)):
            lane = lanes - base
            chosen = (lane >= 0) & (lane < 64) & (rows == lane + 64 * z_lo)
            picked = picked + jnp.dot(
                part, jnp.where(chosen, 1.0, 0.0).astype(BF16), preferred_element_type=F32
            )
    send[:, 0:16, :] = jnp.broadcast_to(direction[None], (send.shape[0], 16, 256))
    send[:, 16:32, :] = jnp.broadcast_to(picked.astype(BF16)[None], (send.shape[0], 16, 256))


def update_kernel(place, received, proj, weights, new_weights, moments):
    direction = received[:, 0:16, :].reshape(256, 256)
    update = lax.dot_general(direction, proj[0], TN, preferred_element_type=F32)
    new_weights[0] = (weights[0].astype(F32) - 0.5 * update).astype(BF16)
    block = place[0] % 8
    rows = lax.broadcasted_iota(jnp.int32, (16, 256), 0)
    lanes = lax.broadcasted_iota(jnp.int32, (16, 256), 1)
    wanted = (rows // 8) * 64 + block * 8 + rows % 8
    chosen = jnp.where(lanes % 128 == wanted, 1.0, 0.0).astype(BF16)
    moments[0] = lax.dot_general(
        chosen, received[:, 16:32, :].reshape(256, 256), NT, preferred_element_type=F32
    )


def shards(grads, weights, first_moment, second_moment, old_seeds, new_seeds):
    layers, _, cols = weights.shape
    rank = first_moment.shape[2]
    half = rank // 16
    spread = math.sqrt(12.0 / rank)
    place = jnp.stack([lax.axis_index("dp"), lax.axis_index("mp")]).astype(jnp.int32)

    state = jnp.concatenate(
        [weights, first_moment.astype(BF16), second_moment.astype(BF16)], axis=2
    )
    state = lax.all_gather(state, "dp", axis=1, tiled=True)

    smem = pl.BlockSpec(memory_space=pltpu.SMEM)
    proj, send = pl.pallas_call(
        functools.partial(project_kernel, rank=rank, cols=cols, spread=spread),
        grid=(layers,),
        in_specs=[
            smem,
            smem,
            smem,
            pl.BlockSpec((1, 1, rank, cols), lambda layer: (0, layer, 0, 0)),
        ],
        out_specs=[
            pl.BlockSpec((1, rank, cols), lambda layer: (layer, 0, 0)),
            pl.BlockSpec((half, 32, rank), lambda layer: (layer, 0, 0)),
        ],
        out_shape=[
            jax.ShapeDtypeStruct((layers, rank, cols), BF16),
            jax.ShapeDtypeStruct((layers * half, 32, rank), BF16),
        ],
        scratch_shapes=[
            pltpu.VMEM((rank, 128), jnp.int32),
            pltpu.VMEM((8, cols), jnp.int32),
            pltpu.VMEM((rank, cols), BF16),
        ],
        compiler_params=pltpu.CompilerParams(vmem_limit_bytes=32 * 2**20),
        name="project",
    )(place, new_seeds, old_seeds, grads)

    received = lax.all_to_all(send, BOTH, 0, 0, axis_index_groups=PLANES, tiled=True)
    send = pl.pallas_call(
        sum_kernel,
        out_shape=jax.ShapeDtypeStruct((16, 32, rank), BF16),
        name="plane_sum",
    )(received)
    received = lax.all_to_all(send, BOTH, 0, 0, axis_index_groups=LINES, tiled=True)

    dp, mp = place[0], place[1]
    x_core, y = dp % 8, mp % 4
    owner = ((x_core // 2) * 4 + y) * 2 + x_core % 2
    place = jnp.stack([dp, mp, owner // half])
    send = pl.pallas_call(
        moment_kernel,
        grid_spec=pltpu.PrefetchScalarGridSpec(
            num_scalar_prefetch=1,
            grid=(1,),
            in_specs=[
                pl.BlockSpec((16, 32, rank), lambda _, where: (0, 0, 0)),
                pl.BlockSpec((1, rank, rank), lambda _, where: (where[2], 0, cols // rank)),
                pl.BlockSpec((1, rank, rank), lambda _, where: (where[2], 0, cols // rank + 1)),
            ],
            out_specs=pl.BlockSpec((32, 32, rank), lambda _, where: (0, 0, 0)),
        ),
        out_shape=jax.ShapeDtypeStruct((32, 32, rank), BF16),
        name="moment",
    )(place, received, state, state)
    received = lax.all_to_all(send, BOTH, 0, 0, axis_index_groups=PLANES, tiled=True)

    new_weights, moments = pl.pallas_call(
        update_kernel,
        grid=(layers,),
        in_specs=[
            smem,
            pl.BlockSpec((half, 32, rank), lambda layer: (layer, 0, 0)),
            pl.BlockSpec((1, rank, cols), lambda layer: (layer, 0, 0)),
            pl.BlockSpec((1, rank, cols), lambda layer: (layer, 0, 0)),
        ],
        out_specs=[
            pl.BlockSpec((1, rank, cols), lambda layer: (layer, 0, 0)),
            pl.BlockSpec((1, 16, rank), lambda layer: (layer, 0, 0)),
        ],
        out_shape=[
            jax.ShapeDtypeStruct((layers, rank, cols), BF16),
            jax.ShapeDtypeStruct((layers, 16, rank), F32),
        ],
        compiler_params=pltpu.CompilerParams(vmem_limit_bytes=32 * 2**20),
        name="update",
    )(place, received, proj, state)
    return new_weights, moments[:, 0:8], moments[:, 8:16]


def solution(mesh):
    placed = (
        P("dp", None, None, "mp"),
        P(None, "dp", "mp"),
        P(None, "dp", None),
        P(None, "dp", None),
        P(),
        P(),
    )
    return jax.shard_map(
        shards,
        mesh=mesh,
        in_specs=placed,
        out_specs=(P(None, None, "mp"), P(None, "dp", None), P(None, "dp", None)),
        check_vma=False,
    )
```

time: 550 us -> 122 us (0.22); the launches traced: 542 us -> 121 us
  waiting for transfers between devices: 246 us -> 26.6 us
  blocking collectives: 184 us -> 42.1 us
  matrix products: 88.2 us -> 0 us
  Pallas kernels: 0 us -> 15.4 us
  starting transfers between devices: 0.74 us -> 13.4 us
    reduce_scatter x2 -> x0, waiting for transfers between devices: 246 us -> none  [shards(): lax.psum_scatter(partial_value, 'dp', scatter_dimension=0, tiled=True)]
    all_gather x2 -> x0, blocking collectives: 99.4 us -> none  [shards(): gathered.append(lax.all_gather(block, 'dp', axis=0, tiled=True))]
    dot_general x10 -> x0, matrix products: 88.2 us -> none  [the longest x4 63.8 us: inner_rank(): lax.dot_general(left, right, (((1,), (1,)), ((), ())), preferred_element_...]
    psum x1 -> x0, blocking collectives: 84.7 us -> none  [shards(): compressed = lax.psum(owned, 'mp')]
    all_to_all x0 -> x2, blocking collectives: none -> 42.1 us  [shards(): lax.all_to_all(send, BOTH, 0, 0, axis_index_groups=PLANES, tiled=True)]
    all_to_all x0 -> x1, waiting for transfers between devices: none -> 19 us  [shards(): lax.all_to_all(send, BOTH, 0, 0, axis_index_groups=LINES, tiled=True)]
    pallas_call x0 -> x4, Pallas kernels: none -> 15.4 us  [the longest x1 7.67 us: shards(): pl.pallas_call(functools.partial(project_kernel, rank=rank, cols=cols, sp...]
    all_to_all x0 -> x1, starting transfers between devices: none -> 13.3 us  [shards(): lax.all_to_all(send, BOTH, 0, 0, axis_index_groups=LINES, tiled=True)]
  transfers between devices with their start and end apart: 3 -> 2, of which waited for: 2 -> 2; matrix products, arithmetic and copies ran while one was open for 10% -> 1% of each run, Pallas kernels for 0% -> 8%
where the time goes in v1:
time: 122 us; the launch traced here: 121 us
  blocking collectives  42.1 us (35%)
  waiting for transfers between devices  26.6 us (22%)
  Pallas kernels  15.4 us (13%)
  between operations  14.1 us (12%)
  starting transfers between devices  13.4 us (11%)
  local copies, waits for them, and re-layouts  6.16 us (5%)
  other arithmetic  3.63 us (3%)
    all_to_all x2, blocking collectives, shards(): lax.all_to_all(send, BOTH, 0, 0, axis_index_groups=PLANES, tiled=True)  42.1 us
    all_to_all x1, waiting for transfers between devices, shards(): lax.all_to_all(send, BOTH, 0, 0, axis_index_groups=LINES, tiled=True)  19 us
    all_to_all x1, starting transfers between devices, shards(): lax.all_to_all(send, BOTH, 0, 0, axis_index_groups=LINES, tiled=True)  13.3 us
    pallas_call x1, Pallas kernels, shards(): pl.pallas_call(functools.partial(project_kernel, rank=rank, cols=cols, sp...  7.67 us
    all_gather x1, waiting for transfers between devices, shards(): state = lax.all_gather(state, 'dp', axis=1, tiled=True)  7.65 us
    unnamed x16, local copies, waits for them, and re-layouts  5.54 us
    pallas_call x1, Pallas kernels, shards(): pl.pallas_call(moment_kernel, grid_spec=pltpu.PrefetchScalarGridSpec(num_...  3.38 us
    pallas_call x1, Pallas kernels, shards(): pl.pallas_call(update_kernel, grid=(layers,), in_specs=[smem, pl.BlockSpe...  2.45 us
  transfers between devices with their start and end apart: 2, of which 2 were waited for; matrix products, arithmetic and copies ran while one was open for 1% of the time, Pallas kernels for 8%

profile of v1, /device:TPU:1, one launch (start us, length us, event | category | flops | bytes accessed | tf_op | source)
XLA Modules:
  0.0 121.4 jit_solution(4717394780753530509)
XLA Ops:
  7.2 0.0 all-gather.2.cloned.1.call-start
  7.2 0.7 convert_element_type.6
  7.9 0.7 convert_element_type.7
  8.7 1.4 %pad_maximum_fusion = bf16[2,8,2304]{2,1,0:T(8,128)(2,1)} fusion(bf16[2,8,256]{2,1,0:T(8,128)(2,1)S(1)} %convert_element_type.7, bf16[2,8,256]{2,1,0:T(8,128)(2,1)S(1)} %convert_element_type.6, bf16[2,8,1792]{2,1,0:T(8,128)(2,1)} %param.7), kind=kLoop, calls=%fused_computation | loop fusion | flops 221184 | bytes 147456 | tf_op jit(solution)/shard_map/concatenate | solution.py:196
  10.1 0.0 all-gather.2.cloned.1.call-update
  10.1 0.1 pad_add_fusion.1.place
  10.2 1.5 %copy-done.3 = bf16[1,2,256,1792]{3,2,1,0:T(8,128)(2,1)S(1)} copy-done((bf16[1,2,256,1792]{3,2,1,0:T(8,128)(2,1)S(1)}, bf16[1,2,256,1792]{3,2,1,0:T(8,128)(2,1)}, u32[]{:S(2)}) %copy-start.3) | copy-done | bytes 1835032
  11.7 0.7 copy-done.5
  12.4 0.7 copy-done.6
  13.0 7.7 %project.1 = (bf16[2,256,1792]{2,1,0:T(8,128)(2,1)S(1)}, bf16[32,32,256]{2,1,0:T(8,128)(2,1)S(1)}) custom-call(s32[2]{0:T(128)S(1)} %pad_add_fusion.1.place, s32[2]{0:T(128)S(1)} %copy-done.5, s32[2]{0:T(128)S(1)} %copy-done.6, bf16[1,2,256,1792]{3,2,1,0:T(8,128)(2,1)S(1)} %copy-done.3), custom_call_target="tpu_custom_call" | custom-call | tf_op jit(solution)/shard_map/project/pallas_call | solution.py:202
  20.7 0.0 copy-start.1
  20.7 1.2 %copy-done.1 = bf16[2,256,1792]{2,1,0:T(8,128)(2,1)} copy-done((bf16[2,256,1792]{2,1,0:T(8,128)(2,1)}, bf16[2,256,1792]{2,1,0:T(8,128)(2,1)S(1)}, u32[]{:S(2)}) %copy-start.1) | copy-done | bytes 1835032
  21.9 23.4 %all_to_all.15.received = bf16[32,32,256]{2,1,0:T(8,128)(2,1)} all-to-all(bf16[32,32,256]{2,1,0:T(8,128)(2,1)S(1)} %get-tuple-element.7), channel_id=1, replica_groups={{0,16,1,17,2,18,3,19,32,48,33,49,34,50,35,51,64,80,65,81,66,82,67,83,96..., dimensions={0} | all-to-all | bytes 1048576 | tf_op jit(solution)/shard_map/all_to_all | solution.py:228
  45.3 1.9 %plane_sum.1 = bf16[16,32,256]{2,1,0:T(8,128)(2,1)} custom-call(bf16[32,32,256]{2,1,0:T(8,128)(2,1)} %all_to_all.15.received), custom_call_target="tpu_custom_call" | custom-call | tf_op jit(solution)/shard_map/plane_sum/pallas_call | solution.py:229
  47.1 13.3 %all-to-all-start.1 = ((bf16[16,32,256]{2,1,0:T(8,128)(2,1)}), bf16[16,32,256]{2,1,0:T(8,128)(2,1)S(1)}, u32[]{:S(2)}, u32[]{:S(2)}) async-start(bf16[16,32,256]{2,1,0:T(8,128)(2,1)} %plane_sum.1), calls=%async_computation.1 | async-start | bytes 524288 | tf_op jit(solution)/shard_map/all_to_all | solution.py:234
  60.6 0.7 pad_add_fusion.place
  61.2 19.0 %all-to-all-done.1.received = bf16[16,32,256]{2,1,0:T(8,128)(2,1)S(1)} async-done(((bf16[16,32,256]{2,1,0:T(8,128)(2,1)}), bf16[16,32,256]{2,1,0:T(8,128)(2,1)S(1)}, u32[]{:S(2)}, u32[]{:S(2)}) %all-to-all-start.1) | async-done | bytes 262176 | tf_op jit(solution)/shard_map/all_to_all | solution.py:234
  80.2 7.6 %all-gather.2.cloned.1.call-done.first_moment.second_moment.weights = bf16[2,256,2304]{2,1,0:T(8,128)(2,1)} async-done(((bf16[2,8,2304]{2,1,0:T(8,128)(2,1)}), bf16[2,256,2304]{2,1,0:T(8,128)(2,1)}) %all-gather.2.cloned.1.call-update) | async-done | bytes 2359312 | tf_op jit(solution)/shard_map/all_gather | solution.py:199
  87.9 0.0 copy-done.7
  87.9 3.4 %moment.1 = bf16[32,32,256]{2,1,0:T(8,128)(2,1)} custom-call(s32[3]{0:T(128)} %pad_add_fusion.place, bf16[16,32,256]{2,1,0:T(8,128)(2,1)} %copy-done.7, bf16[2,256,2304]{2,1,0:T(8,128)(2,1)} %all-gather.2.cloned.1.call-done.first_moment.second_moment.weights, bf16[2,256,2304]{2,1,0:T(8,128)(2,1)} %all-gather.2.cloned.1.call-done.first_moment.second_moment.weights), custom_call_target="tpu_custom_call" | custom-call | tf_op jit(solution)/shard_map/moment/pallas_call | solution.py:240
  91.2 18.7 %all_to_all.16.received = bf16[32,32,256]{2,1,0:T(8,128)(2,1)S(1)} all-to-all(bf16[32,32,256]{2,1,0:T(8,128)(2,1)} %moment.1), channel_id=1, replica_groups={{0,16,1,17,2,18,3,19,32,48,33,49,34,50,35,51,64,80,65,81,66,82,67,83,96..., dimensions={0} | all-to-all | bytes 1048576 | tf_op jit(solution)/shard_map/all_to_all | solution.py:255
  110.0 1.5 %copy-done.2 = bf16[2,256,1792]{2,1,0:T(8,128)(2,1)S(1)} copy-done((bf16[2,256,1792]{2,1,0:T(8,128)(2,1)S(1)}, bf16[2,256,1792]{2,1,0:T(8,128)(2,1)}, u32[]{:S(2)}) %copy-start.2) | copy-done | bytes 1835032
  111.5 2.4 %update.1 = (bf16[2,256,1792]{2,1,0:T(8,128)(2,1)}, f32[2,16,256]{2,1,0:T(8,128)S(1)}) custom-call(s32[3]{0:T(128)S(1)} %copy-done.4, bf16[32,32,256]{2,1,0:T(8,128)(2,1)S(1)} %all_to_all.16.received, bf16[2,256,1792]{2,1,0:T(8,128)(2,1)S(1)} %copy-done.2, bf16[2,256,2304]{2,1,0:T(8,128)(2,1)S(1)} %copy-done), custom_call_target="tpu_custom_call" | custom-call | tf_op jit(solution)/shard_map/update/pallas_call | solution.py:257
  113.9 0.6 fusion
  (9 shorter events, 0.0 us)
Async XLA Ops:
  7.2 80.7 %all-gather.2.cloned.1.call-start = ((), (), s32[]{:S(2)}) async-start(), calls=%async_computation.3 | async-start | bytes 2433024 | tf_op jit(solution)/shard_map/all_gather | solution.py:199
  10.2 1.5 %copy-start.3 = (bf16[1,2,256,1792]{3,2,1,0:T(8,128)(2,1)S(1)}, bf16[1,2,256,1792]{3,2,1,0:T(8,128)(2,1)}, u32[]{:S(2)}) copy-start(bf16[1,2,256,1792]{3,2,1,0:T(8,128)(2,1)} %grads.1) | copy-start | bytes 5505028
  11.7 0.7 copy-start.5
  12.4 0.7 copy-start.6
  20.7 1.2 %copy-start.1 = (bf16[2,256,1792]{2,1,0:T(8,128)(2,1)}, bf16[2,256,1792]{2,1,0:T(8,128)(2,1)S(1)}, u32[]{:S(2)}) copy-start(bf16[2,256,1792]{2,1,0:T(8,128)(2,1)S(1)} %get-tuple-element.8.proj) | copy-start | bytes 5505028
  47.1 33.1 %all-to-all-start.1 = ((bf16[16,32,256]{2,1,0:T(8,128)(2,1)}), bf16[16,32,256]{2,1,0:T(8,128)(2,1)S(1)}, u32[]{:S(2)}, u32[]{:S(2)}) async-start(bf16[16,32,256]{2,1,0:T(8,128)(2,1)} %plane_sum.1), calls=%async_computation.1 | async-start | bytes 524288 | tf_op jit(solution)/shard_map/all_to_all | solution.py:234
  61.2 48.7 %copy-start.4 = (s32[3]{0:T(128)S(1)}, s32[3]{0:T(128)}, u32[]{:S(2)}) copy-start(s32[3]{0:T(128)} %pad_add_fusion.place) | copy-start | bytes 40
  80.2 7.7 %copy-start.7 = (bf16[16,32,256]{2,1,0:T(8,128)(2,1)}, bf16[16,32,256]{2,1,0:T(8,128)(2,1)S(1)}, u32[]{:S(2)}) copy-start(bf16[16,32,256]{2,1,0:T(8,128)(2,1)S(1)} %all-to-all-done.1.received) | copy-start | bytes 786436
  87.9 22.1 %copy-start = (bf16[2,256,2304]{2,1,0:T(8,128)(2,1)S(1)}, bf16[2,256,2304]{2,1,0:T(8,128)(2,1)}, u32[]{:S(2)}) copy-start(bf16[2,256,2304]{2,1,0:T(8,128)(2,1)} %all-gather.2.cloned.1.call-done.first_moment.second_moment.weights) | copy-start | bytes 7077892
  110.0 1.5 %copy-start.2 = (bf16[2,256,1792]{2,1,0:T(8,128)(2,1)S(1)}, bf16[2,256,1792]{2,1,0:T(8,128)(2,1)}, u32[]{:S(2)}) copy-start(bf16[2,256,1792]{2,1,0:T(8,128)(2,1)} %copy-done.1) | copy-start | bytes 5505028
Sparse Core Ops, SparseCore 0:
  10.2 77.5 all-gather.1

commit v2 on v0

v2 whole, which is shorter than its diff:
```python
import functools
import math

import jax
import jax.numpy as jnp
from jax import lax
from jax.experimental import pallas as pl
from jax.experimental.pallas import tpu as pltpu
from jax.sharding import PartitionSpec as P

PRIME = 65521
CUT = 46000
F32 = jnp.float32
BF16 = jnp.bfloat16
BOTH = ("dp", "mp")
NT = (((1,), (1,)), ((), ()))
TN = (((0,), (0,)), ((), ()))
HIGHEST = lax.Precision.HIGHEST


FOUR = range(4)
TWO = range(2)


def device(z, x, core, y):
    return ((z % 4 * 4 + x) * 2 + core) * 16 + z // 4 * 4 + y


SLABS = [
    [device(2 * pair + odd, x, core, y) for odd in TWO for x in FOUR for y in FOUR for core in TWO]
    for pair in range(8)
]
LINES = [
    [device(2 * pair + odd, x, core, y) for pair in range(8)]
    for odd in TWO
    for x in FOUR
    for y in FOUR
    for core in TWO
]


def copy_index(z_lo, x, core):
    return (z_lo * 4 + x) * 2 + core


def swap(z, x, core):
    return [
        (copy_index(a, b, c), copy_index(a ^ z, b ^ x, c ^ core))
        for a in FOUR
        for b in FOUR
        for c in TWO
    ]


def below(values, bound):
    return jnp.where(values >= bound, values - bound, values)


def fold(values):
    return values - PRIME * (values >> 16)


def product(values):
    return below(values, CUT) * ((values >> 1) + 1)


def scrambled(values):
    return below(fold(fold(product(values) + 12345)), PRIME)


def row_keys(offset, rank_ids):
    return below(fold(rank_ids * 251 + offset * 3), PRIME)


def column_keys(offset, columns):
    return below(2 * scrambled(below(fold(columns * 7 + offset), PRIME)), PRIME)


def entries(keys, keys_later, columns2, spread):
    first = fold(product(below(keys + columns2, PRIME)))
    second = below(fold(first * 3 + keys_later), PRIME)
    last = fold(product(second) + 12345).astype(F32)
    whole = jnp.floor((last + 0.5) * (1.0 / PRIME))
    return (((last - 32760.0) - whole * float(PRIME)) * (spread / PRIME)).astype(BF16)


def project_kernel(
    place,
    grads_hbm,
    first_moment,
    second_moment,
    weights,
    proj_hbm,
    send,
    weights_out,
    grads,
    proj,
    keys,
    columns2,
    old_rows,
    load_sems,
    store_sems,
    *,
    spread,
):
    layers, rank, cols = proj.shape
    dp, mp = place[0], place[1]
    tiles = cols // 128
    share = 64 // layers
    loads = [
        pltpu.make_async_copy(grads_hbm.at[0, layer], grads.at[layer], load_sems.at[layer])
        for layer in range(layers)
    ]
    stores = [
        pltpu.make_async_copy(proj.at[layer], proj_hbm.at[layer], store_sems.at[layer])
        for layer in range(layers)
    ]
    for load in loads:
        load.start()
    weights_out[...] = weights[...]
    lanes = lax.broadcasted_iota(jnp.int32, (8, cols), 1) + mp * cols
    row = lax.broadcasted_iota(jnp.int32, (rank, 128), 0)

    def both_halves(eight):
        return jnp.concatenate([eight, eight], axis=0)

    y = mp % 4
    for layer in range(layers):
        group = slice(share * layer, share * layer + share)
        offset = lax.rem(place[2 + layer], PRIME)
        keys[...] = row_keys(offset, row)
        columns2[...] = column_keys(offset, lanes)

        def chunk(index, _, layer=layer):
            at = pl.multiple_of(index * 16, 16)
            mine = keys[pl.ds(at, 16), :]
            later = below(mine + 3 * 12345, PRIME)
            for tile in range(tiles):
                cut = slice(tile * 128, tile * 128 + 128)
                proj[layer, pl.ds(at, 16), cut] = entries(
                    mine, later, both_halves(columns2[:, cut]), spread
                )
            return 0

        lax.fori_loop(0, rank // 16, chunk, 0)
        stores[layer].start()
        loads[layer].wait()
        compressed = lax.dot_general(proj[layer], grads[layer], NT, preferred_element_type=F32)
        send[group, :, 0:rank] = compressed.reshape(share, 8, rank).astype(BF16)
        moments = jnp.where(y < 2, first_moment[layer], second_moment[layer])
        half = jnp.where(y % 2 == 0, moments[:, 0:128], moments[:, 128:256])
        send[group, :, 2 * rank : 2 * rank + 128] = jnp.broadcast_to(
            half[None], (share, 8, 128)
        ).astype(BF16)

        mine_layer = dp // (rank // 16)

        @pl.when(mine_layer == layer)
        def _(layer=layer, group=group):
            old_rows[...] = jnp.zeros_like(old_rows)
            old_offset = lax.rem(place[4 + layer], PRIME)
            at = pl.multiple_of((dp % (rank // 16)) * 16, 16)
            mine = row_keys(old_offset, lax.broadcasted_iota(jnp.int32, (16, 128), 0) + at)
            later = below(mine + 3 * 12345, PRIME)
            columns2[...] = column_keys(old_offset, lanes)
            for tile in range(tiles):
                cut = slice(tile * 128, tile * 128 + 128)
                old_rows[pl.ds(at, 16), cut] = entries(
                    mine, later, both_halves(columns2[:, cut]), spread
                )
            gram = lax.dot_general(proj[layer], old_rows[...], NT, preferred_element_type=F32)
            send[group, :, rank : 2 * rank] = gram.reshape(share, 8, rank).astype(BF16)

        @pl.when(mine_layer != layer)
        def _(group=group):
            send[group, :, rank : 2 * rank] = jnp.zeros((share, 8, rank), BF16)

    for store in stores:
        store.wait()


def summed(received, width):
    total = received[0, :, 0:width].astype(F32)
    for part in range(1, received.shape[0]):
        total = total + received[part, :, 0:width].astype(F32)
    return total


def sum_kernel(received, send, moments):
    send[...] = jnp.broadcast_to(summed(received, 512)[None], send.shape).astype(BF16)
    for chip in range(8):
        for y in FOUR:
            from_core = [received[(chip * 4 + y) * 2 + core, :, 512:640].astype(F32) for core in TWO]
            lanes = slice(y % 2 * 128, y % 2 * 128 + 128)
            moments[y // 2, chip * 16 : chip * 16 + 16, lanes] = jnp.concatenate(
                from_core, axis=0
            ).astype(BF16)


def join_kernel(*refs):
    *pieces, _, joined = refs
    for slot, piece in enumerate(pieces):
        joined[slot] = piece[...]


def moment_kernel(place, received, near, far, *refs):
    send = refs[-1]
    total = summed(received, 512)
    compressed, gram = total[:, 0:256], total[:, 256:512]
    upper = (place[0] // 16) == 1

    def times(left, which):
        near_part, far_part = near[which].astype(F32), far[which].astype(F32)
        return jnp.concatenate(
            [
                lax.dot_general(
                    left, rows, NT, precision=HIGHEST, preferred_element_type=F32
                )
                for rows in (
                    jnp.where(upper, far_part, near_part),
                    jnp.where(upper, near_part, far_part),
                )
            ],
            axis=1,
        )

    first = 0.9 * times(gram, 0) + 0.1 * compressed
    second = 0.95 * times(gram * gram, 1) + 0.05 * compressed * compressed
    direction = first / (jnp.sqrt(second) + 1e-08)
    send[:, :, 0:256] = jnp.broadcast_to(direction[None], (64, 8, 256)).astype(BF16)
    mine = [jnp.where(upper, value[:, 128:256], value[:, 0:128]) for value in (first, second)]
    high = [value.astype(BF16).astype(F32) for value in mine]
    parts = high + [value - top for value, top in zip(mine, high)]
    lane = lax.broadcasted_iota(jnp.int32, (8, 128), 1)
    for quarter in FOUR:
        packed = pltpu.roll(parts[0], (128 - 32 * quarter) % 128, 1)
        for slot in (1, 2, 3):
            moved = pltpu.roll(parts[slot], (32 * slot - 32 * quarter) % 128, 1)
            packed = jnp.where(lane >= 32 * slot, moved, packed)
        send[16 * quarter : 16 * quarter + 16, :, 256:384] = jnp.broadcast_to(
            packed[None], (16, 8, 128)
        ).astype(BF16)


def update_kernel(place, received, proj, *refs):
    own, other = refs[0:4], refs[4:8]
    new_weights, new_first, new_second, update = refs[8:]
    dp = place[0]
    z, x, core = dp // 8, dp // 2 % 4, dp % 2
    cols = proj.shape[2]
    direction = received[:, :, 0:256].astype(F32).reshape(256, 256).astype(BF16)
    update[...] = 0.5 * lax.dot_general(direction, proj[0], TN, preferred_element_type=F32)
    for x_bits in FOUR:
        for z_bits in FOUR:
            at = pl.multiple_of((z ^ z_bits) * 64 + (x ^ x_bits) * 16, 16)
            mine = own[x_bits][z_bits, 0].astype(F32)
            theirs = other[x_bits][z_bits, 0].astype(F32)
            low = jnp.where(core == 0, mine, theirs)
            high = jnp.where(core == 0, theirs, mine)
            block = jnp.concatenate([low, high], axis=0)
            new_weights[0, pl.ds(at, 16), :] = (block - update[pl.ds(at, 16), :]).astype(BF16)
    rows = lax.broadcasted_iota(jnp.int32, (16, 128), 0)
    lanes = lax.broadcasted_iota(jnp.int32, (16, 128), 1)
    wanted = rows // 8 * 32 + x % 2 * 16 + core * 8 + rows % 8
    chosen = jnp.where(lanes % 64 == wanted, 1.0, 0.0).astype(BF16)
    moments = lax.dot_general(
        chosen,
        received[:, :, 256:384].astype(F32).reshape(256, 128).astype(BF16),
        NT,
        preferred_element_type=F32,
    )
    new_first[0] = moments[0:8]
    new_second[0] = moments[8:16]


def shards(grads, weights, first_moment, second_moment, old_seeds, new_seeds):
    layers, block, cols = weights.shape
    rank = first_moment.shape[2]
    spread = math.sqrt(12.0 / rank)
    place = jnp.concatenate(
        [jnp.stack([lax.axis_index("dp"), lax.axis_index("mp")]).astype(jnp.int32), new_seeds, old_seeds]
    )
    smem = pl.BlockSpec(memory_space=pltpu.SMEM)
    vmem = pl.BlockSpec(memory_space=pltpu.VMEM)
    hbm = pl.BlockSpec(memory_space=pltpu.HBM)
    anywhere = pl.BlockSpec(memory_space=pl.ANY)
    roomy = pltpu.CompilerParams(vmem_limit_bytes=56 * 2**20)
    small = pltpu.CompilerParams(vmem_limit_bytes=8 * 2**20)

    proj, send, weights = pl.pallas_call(
        functools.partial(project_kernel, spread=spread),
        in_specs=[smem, hbm, vmem, vmem, vmem],
        out_specs=[hbm, vmem, vmem],
        out_shape=[
            jax.ShapeDtypeStruct((layers, rank, cols), BF16),
            jax.ShapeDtypeStruct((64, 8, 640), BF16),
            jax.ShapeDtypeStruct(weights.shape, BF16),
        ],
        scratch_shapes=[
            pltpu.VMEM((layers, rank, cols), BF16),
            pltpu.VMEM((layers, rank, cols), BF16),
            pltpu.VMEM((rank, 128), jnp.int32),
            pltpu.VMEM((8, cols), jnp.int32),
            pltpu.VMEM((rank, cols), BF16),
            pltpu.SemaphoreType.DMA((layers,)),
            pltpu.SemaphoreType.DMA((layers,)),
        ],
        compiler_params=roomy,
        cost_estimate=pl.CostEstimate(
            flops=8 * 10**9, bytes_accessed=6 * 10**6, transcendentals=0
        ),
        name="project",
    )(place, grads, first_moment, second_moment, weights)

    received = lax.all_to_all(send, BOTH, 0, 0, axis_index_groups=SLABS, tiled=True)
    column = [weights] + [lax.ppermute(weights, "dp", swap(bits, 0, 0)) for bits in (1, 2, 3)]
    send, near = pl.pallas_call(
        sum_kernel,
        in_specs=[vmem],
        out_specs=[vmem, vmem],
        out_shape=[
            jax.ShapeDtypeStruct((8, 8, 2 * rank), BF16),
            jax.ShapeDtypeStruct((2, rank // 2, rank), BF16),
        ],
        compiler_params=small,
        name="slab_sum",
    )(received)
    received = lax.all_to_all(send, BOTH, 0, 0, axis_index_groups=LINES, tiled=True)
    far = lax.ppermute(near, "dp", swap(2, 0, 0))
    column = pl.pallas_call(
        join_kernel,
        in_specs=[vmem] * 4 + [anywhere],
        out_specs=vmem,
        out_shape=jax.ShapeDtypeStruct((4, *weights.shape), BF16),
        compiler_params=small,
        name="join",
    )(*column, near)
    own = [column] + [lax.ppermute(column, "dp", swap(0, bits, 0)) for bits in (1, 2, 3)]
    send = pl.pallas_call(
        moment_kernel,
        in_specs=[smem, vmem, vmem, vmem] + [anywhere] * 3,
        out_specs=vmem,
        out_shape=jax.ShapeDtypeStruct((64, 8, 384), BF16),
        compiler_params=small,
        name="moment",
    )(place, received, near, far, *own[1:])
    received = lax.all_to_all(send, BOTH, 0, 0, axis_index_groups=SLABS, tiled=True)
    other = [lax.ppermute(piece, "dp", swap(0, 0, 1)) for piece in own]

    whole = pl.BlockSpec((1, rank, cols), lambda layer: (layer, 0, 0))
    piece = pl.BlockSpec((4, 1, block, cols), lambda layer: (0, layer, 0, 0))
    rows = pl.BlockSpec((1, block, rank), lambda layer: (layer, 0, 0))
    return pl.pallas_call(
        update_kernel,
        grid=(layers,),
        in_specs=[
            smem,
            pl.BlockSpec((64 // layers, 8, 384), lambda layer: (layer, 0, 0)),
            whole,
        ]
        + [piece] * 8,
        out_specs=[whole, rows, rows],
        out_shape=[
            jax.ShapeDtypeStruct((layers, rank, cols), BF16),
            jax.ShapeDtypeStruct((layers, block, rank), F32),
            jax.ShapeDtypeStruct((layers, block, rank), F32),
        ],
        scratch_shapes=[pltpu.VMEM((rank, cols), F32)],
        compiler_params=pltpu.CompilerParams(vmem_limit_bytes=56 * 2**20),
        name="update",
    )(place, received, proj, *own, *other)


def solution(mesh):
    placed = (
        P("dp", None, None, "mp"),
        P(None, "dp", "mp"),
        P(None, "dp", None),
        P(None, "dp", None),
        P(),
        P(),
    )
    return jax.shard_map(
        shards,
        mesh=mesh,
        in_specs=placed,
        out_specs=(P(None, None, "mp"), P(None, "dp", None), P(None, "dp", None)),
        check_vma=False,
    )
```

time: 550 us -> 92.7 us (0.17); the launches traced: 542 us -> 91.9 us
  waiting for transfers between devices: 246 us -> 12.8 us
  blocking collectives: 184 us -> 0 us
  matrix products: 88.2 us -> 0 us
  starting transfers between devices: 0.74 us -> 60.3 us
  between operations: 18.6 us -> 0.95 us
  Pallas kernels: 0 us -> 15.8 us
    reduce_scatter x2 -> x0, waiting for transfers between devices: 246 us -> none  [shards(): lax.psum_scatter(partial_value, 'dp', scatter_dimension=0, tiled=True)]
    all_gather x2 -> x0, blocking collectives: 99.4 us -> none  [shards(): gathered.append(lax.all_gather(block, 'dp', axis=0, tiled=True))]
    dot_general x10 -> x0, matrix products: 88.2 us -> none  [the longest x4 63.8 us: inner_rank(): lax.dot_general(left, right, (((1,), (1,)), ((), ())), preferred_element_...]
    psum x1 -> x0, blocking collectives: 84.7 us -> none  [shards(): compressed = lax.psum(owned, 'mp')]
    ppermute x0 -> x11, starting transfers between devices: none -> 31.2 us  [the longest x3 9.27 us: shards(): lax.ppermute(weights, 'dp', swap(bits, 0, 0))]
    all_to_all x0 -> x3, starting transfers between devices: none -> 29.1 us  [the longest x2 15.8 us: shards(): lax.all_to_all(send, BOTH, 0, 0, axis_index_groups=SLABS, tiled=True)]
    pallas_call x0 -> x5, Pallas kernels: none -> 15.8 us  [the longest x1 9.32 us: shards(): pl.pallas_call(functools.partial(project_kernel, spread=spread), in_specs...]
    ppermute x0 -> x11, waiting for transfers between devices: none -> 7.84 us  [the longest x1 6.42 us: shards(): far = lax.ppermute(near, 'dp', swap(2, 0, 0))]
  transfers between devices with their start and end apart: 3 -> 14, of which waited for: 2 -> 4; matrix products, arithmetic and copies ran while one was open for 10% -> 0% of each run, Pallas kernels for 0% -> 1%
where the time goes in v2:
time: 92.7 us; the launch traced here: 91.9 us
  starting transfers between devices  60.3 us (65%)
  Pallas kernels  15.8 us (17%)
  waiting for transfers between devices  12.8 us (14%)
  other arithmetic  1.33 us (1%)
  between operations  0.95 us (1%)
    all_to_all x2, starting transfers between devices, shards(): lax.all_to_all(send, BOTH, 0, 0, axis_index_groups=SLABS, tiled=True)  15.8 us
    all_to_all x1, starting transfers between devices, shards(): lax.all_to_all(send, BOTH, 0, 0, axis_index_groups=LINES, tiled=True)  13.2 us
    pallas_call x1, Pallas kernels, shards(): pl.pallas_call(functools.partial(project_kernel, spread=spread), in_specs...  9.32 us
    ppermute x3, starting transfers between devices, shards(): lax.ppermute(weights, 'dp', swap(bits, 0, 0))  9.27 us
    ppermute x3, starting transfers between devices, shards(): lax.ppermute(column, 'dp', swap(0, bits, 0))  8.98 us
    ppermute x4, starting transfers between devices, shards(): other = [lax.ppermute(piece, 'dp', swap(0, 0, 1)) for piece in own]  8.72 us
    ppermute x1, waiting for transfers between devices, shards(): far = lax.ppermute(near, 'dp', swap(2, 0, 0))  6.42 us
    all_to_all x2, waiting for transfers between devices, shards(): lax.all_to_all(send, BOTH, 0, 0, axis_index_groups=SLABS, tiled=True)  5.01 us
  transfers between devices with their start and end apart: 14, of which 4 were waited for; matrix products, arithmetic and copies ran while one was open for 0% of the time, Pallas kernels for 1%

profile of v2, /device:TPU:1, one launch (start us, length us, event | category | flops | bytes accessed | tf_op | source)
XLA Modules:
  0.0 91.9 jit_solution(12270073675019790325)
XLA Ops:
  0.6 1.3 %pad_add_fusion.place = s32[6]{0:T(128)} fusion(s32[2]{0:T(128)} %param.10, s32[2]{0:T(128)} %param.11, s32[1]{0:T(128)} %bitcast.1, s32[1]{0:T(128)} %bitcast), kind=kLoop, calls=%fused_computation | loop fusion | flops 18 | bytes 48 | tf_op jit(solution)/shard_map/concatenate | solution.py:280
  2.0 9.3 %project.1 = (bf16[2,256,1792]{2,1,0:T(8,128)(2,1)}, bf16[64,8,640]{2,1,0:T(8,128)(2,1)}, bf16[2,8,1792]{2,1,0:T(8,128)(2,1)}) custom-call(s32[6]{0:T(128)} %pad_add_fusion.place, bf16[1,2,256,1792]{3,2,1,0:T(8,128)(2,1)} %grads_hbm.1, f32[2,8,256]{2,1,0:T(8,128)} %first_moment.1, f32[2,8,256]{2,1,0:T(8,128)} %second_moment.1, bf16[2,8,1792]{2,1,0:T(8,128)(2,1)} %weights.1), custom_call_target="tpu_custom_call" | custom-call | flops 8000000000 | bytes 6000000 | tf_op jit(solution)/shard_map/project/pallas_call | solution.py:290
  11.3 11.0 %all-to-all-start = ((bf16[64,8,640]{2,1,0:T(8,128)(2,1)}), bf16[64,8,640]{2,1,0:T(8,128)(2,1)S(1)}, u32[]{:S(2)}, u32[]{:S(2)}) async-start(bf16[64,8,640]{2,1,0:T(8,128)(2,1)} %get-tuple-element.8), calls=%async_computation | async-start | bytes 1310720 | tf_op jit(solution)/shard_map/all_to_all | solution.py:315
  22.3 5.0 %collective-permute-start.3 = (bf16[2,8,1792]{2,1,0:T(8,128)(2,1)}, bf16[2,8,1792]{2,1,0:T(8,128)(2,1)S(1)}, u32[]{:S(2)}, u32[]{:S(2)}) collective-permute-start(bf16[2,8,1792]{2,1,0:T(8,128)(2,1)} %get-tuple-element.11.refs_0_), channel_id=1, source_target_pairs={{0,384},{16,400},{32,416},{48,432},{64,448},{80,464},{96,480},{112... | collective-permute-start | bytes 172040 | tf_op jit(solution)/shard_map/ppermute | solution.py:316
  27.3 1.9 %collective-permute-start.2 = (bf16[2,8,1792]{2,1,0:T(8,128)(2,1)}, bf16[2,8,1792]{2,1,0:T(8,128)(2,1)S(1)}, u32[]{:S(2)}, u32[]{:S(2)}) collective-permute-start(bf16[2,8,1792]{2,1,0:T(8,128)(2,1)} %get-tuple-element.11.refs_0_), channel_id=1, source_target_pairs={{0,256},{16,272},{32,288},{48,304},{64,320},{80,336},{96,352},{112... | collective-permute-start | bytes 172040 | tf_op jit(solution)/shard_map/ppermute | solution.py:316
  29.2 2.3 %collective-permute-start.1 = (bf16[2,8,1792]{2,1,0:T(8,128)(2,1)}, bf16[2,8,1792]{2,1,0:T(8,128)(2,1)S(1)}, u32[]{:S(2)}, u32[]{:S(2)}) collective-permute-start(bf16[2,8,1792]{2,1,0:T(8,128)(2,1)} %get-tuple-element.11.refs_0_), channel_id=1, source_target_pairs={{0,128},{16,144},{32,160},{48,176},{64,192},{80,208},{96,224},{112... | collective-permute-start | bytes 172040 | tf_op jit(solution)/shard_map/ppermute | solution.py:316
  31.6 4.2 %all-to-all-done.received = bf16[64,8,640]{2,1,0:T(8,128)(2,1)S(1)} async-done(((bf16[64,8,640]{2,1,0:T(8,128)(2,1)}), bf16[64,8,640]{2,1,0:T(8,128)(2,1)S(1)}, u32[]{:S(2)}, u32[]{:S(2)}) %all-to-all-start) | async-done | bytes 655392 | tf_op jit(solution)/shard_map/all_to_all | solution.py:315
  35.8 0.7 slab_sum.1
  36.5 13.2 %all-to-all-start.1 = ((bf16[8,8,512]{2,1,0:T(8,128)(2,1)}), bf16[8,8,512]{2,1,0:T(8,128)(2,1)S(1)}, u32[]{:S(2)}, u32[]{:S(2)}) async-start(bf16[8,8,512]{2,1,0:T(8,128)(2,1)} %get-tuple-element.9), calls=%async_computation.1 | async-start | bytes 131072 | tf_op jit(solution)/shard_map/all_to_all | solution.py:328
  49.8 2.7 %collective-permute-start.6 = (bf16[4,2,8,1792]{3,2,1,0:T(8,128)(2,1)S(1)}, bf16[4,2,8,1792]{3,2,1,0:T(8,128)(2,1)S(1)}, u32[]{:S(2)}, u32[]{:S(2)}) collective-permute-start(bf16[4,2,8,1792]{3,2,1,0:T(8,128)(2,1)S(1)} %join.1.refs_0_), channel_id=1, source_target_pairs={{0,96},{16,112},{32,64},{48,80},{64,32},{80,48},{96,0},{112,16},{1... | collective-permute-start | bytes 688136 | tf_op jit(solution)/shard_map/ppermute | solution.py:338
  52.5 3.1 %collective-permute-start.5 = (bf16[4,2,8,1792]{3,2,1,0:T(8,128)(2,1)S(1)}, bf16[4,2,8,1792]{3,2,1,0:T(8,128)(2,1)S(1)}, u32[]{:S(2)}, u32[]{:S(2)}) collective-permute-start(bf16[4,2,8,1792]{3,2,1,0:T(8,128)(2,1)S(1)} %join.1.refs_0_), channel_id=1, source_target_pairs={{0,64},{16,80},{32,96},{48,112},{64,0},{80,16},{96,32},{112,48},{1... | collective-permute-start | bytes 688136 | tf_op jit(solution)/shard_map/ppermute | solution.py:338
  55.6 3.2 %collective-permute-start.4 = (bf16[4,2,8,1792]{3,2,1,0:T(8,128)(2,1)S(1)}, bf16[4,2,8,1792]{3,2,1,0:T(8,128)(2,1)S(1)}, u32[]{:S(2)}, u32[]{:S(2)}) collective-permute-start(bf16[4,2,8,1792]{3,2,1,0:T(8,128)(2,1)S(1)} %join.1.refs_0_), channel_id=1, source_target_pairs={{0,32},{16,48},{32,0},{48,16},{64,96},{80,112},{96,64},{112,80},{1... | collective-permute-start | bytes 688136 | tf_op jit(solution)/shard_map/ppermute | solution.py:338
  58.8 4.3 %collective-permute-start = (bf16[2,128,256]{2,1,0:T(8,128)(2,1)S(1)}, bf16[2,128,256]{2,1,0:T(8,128)(2,1)S(1)}, u32[]{:S(2)}, u32[]{:S(2)}) collective-permute-start(bf16[2,128,256]{2,1,0:T(8,128)(2,1)S(1)} %get-tuple-element.10.refs_4_.near), channel_id=1, source_target_pairs={{0,256},{16,272},{32,288},{48,304},{64,320},{80,336},{96,352},{112... | collective-permute-start | bytes 393224 | tf_op jit(solution)/shard_map/ppermute | solution.py:329
  63.1 6.4 %collective-permute-done.far = bf16[2,128,256]{2,1,0:T(8,128)(2,1)S(1)} collective-permute-done((bf16[2,128,256]{2,1,0:T(8,128)(2,1)S(1)}, bf16[2,128,256]{2,1,0:T(8,128)(2,1)S(1)}, u32[]{:S(2)}, u32[]{:S(2)}) %collective-permute-start) | collective-permute-done | bytes 131104 | tf_op jit(solution)/shard_map/ppermute | solution.py:329
  69.5 1.9 %moment.1 = bf16[64,8,384]{2,1,0:T(8,128)(2,1)} custom-call(s32[6]{0:T(128)S(1)} %copy-done.5, bf16[8,8,512]{2,1,0:T(8,128)(2,1)S(1)} %all-to-all-done.1.received, bf16[2,128,256]{2,1,0:T(8,128)(2,1)S(1)} %get-tuple-element.10.refs_4_.near, bf16[2,128,256]{2,1,0:T(8,128)(2,1)S(1)} %collective-permute-done.far, ...), custom_call_target="tpu_custom_call" | custom-call | tf_op jit(solution)/shard_map/moment/pallas_call | solution.py:339
  71.5 4.9 %all-to-all-start.2 = ((bf16[64,8,384]{2,1,0:T(8,128)(2,1)}), bf16[64,8,384]{2,1,0:T(8,128)(2,1)S(1)}, u32[]{:S(2)}, u32[]{:S(2)}) async-start(bf16[64,8,384]{2,1,0:T(8,128)(2,1)} %moment.1), calls=%async_computation.2 | async-start | bytes 786432 | tf_op jit(solution)/shard_map/all_to_all | solution.py:347
  76.4 2.5 %collective-permute-start.7 = (bf16[4,2,8,1792]{3,2,1,0:T(8,128)(2,1)S(1)}, bf16[4,2,8,1792]{3,2,1,0:T(8,128)(2,1)S(1)}, u32[]{:S(2)}, u32[]{:S(2)}) collective-permute-start(bf16[4,2,8,1792]{3,2,1,0:T(8,128)(2,1)S(1)} %join.1.refs_0_), channel_id=1, source_target_pairs={{0,16},{16,0},{32,48},{48,32},{64,80},{80,64},{96,112},{112,96},{1... | collective-permute-start | bytes 688136 | tf_op jit(solution)/shard_map/ppermute | solution.py:348
  78.8 1.9 %collective-permute-start.10 = (bf16[4,2,8,1792]{3,2,1,0:T(8,128)(2,1)S(1)}, bf16[4,2,8,1792]{3,2,1,0:T(8,128)(2,1)S(1)}, u32[]{:S(2)}, u32[]{:S(2)}) collective-permute-start(bf16[4,2,8,1792]{3,2,1,0:T(8,128)(2,1)S(1)} %collective-permute-done.6.refs_2_.refs_3_), channel_id=1, source_target_pairs={{0,16},{16,0},{32,48},{48,32},{64,80},{80,64},{96,112},{112,96},{1... | collective-permute-start | bytes 688136 | tf_op jit(solution)/shard_map/ppermute | solution.py:348
  80.8 2.4 %collective-permute-start.9 = (bf16[4,2,8,1792]{3,2,1,0:T(8,128)(2,1)S(1)}, bf16[4,2,8,1792]{3,2,1,0:T(8,128)(2,1)S(1)}, u32[]{:S(2)}, u32[]{:S(2)}) collective-permute-start(bf16[4,2,8,1792]{3,2,1,0:T(8,128)(2,1)S(1)} %collective-permute-done.5.refs_1_.refs_2_), channel_id=1, source_target_pairs={{0,16},{16,0},{32,48},{48,32},{64,80},{80,64},{96,112},{112,96},{1... | collective-permute-start | bytes 688136 | tf_op jit(solution)/shard_map/ppermute | solution.py:348
  83.2 1.9 %collective-permute-start.8 = (bf16[4,2,8,1792]{3,2,1,0:T(8,128)(2,1)S(1)}, bf16[4,2,8,1792]{3,2,1,0:T(8,128)(2,1)S(1)}, u32[]{:S(2)}, u32[]{:S(2)}) collective-permute-start(bf16[4,2,8,1792]{3,2,1,0:T(8,128)(2,1)S(1)} %collective-permute-done.4.refs_0_.refs_1_), channel_id=1, source_target_pairs={{0,16},{16,0},{32,48},{48,32},{64,80},{80,64},{96,112},{112,96},{1... | collective-permute-start | bytes 688136 | tf_op jit(solution)/shard_map/ppermute | solution.py:348
  85.2 1.4 %collective-permute-done.8.refs_5_ = bf16[4,2,8,1792]{3,2,1,0:T(8,128)(2,1)S(1)} collective-permute-done((bf16[4,2,8,1792]{3,2,1,0:T(8,128)(2,1)S(1)}, bf16[4,2,8,1792]{3,2,1,0:T(8,128)(2,1)S(1)}, u32[]{:S(2)}, u32[]{:S(2)}) %collective-permute-start.8) | collective-permute-done | bytes 229408 | tf_op jit(solution)/shard_map/ppermute | solution.py:348
  86.6 0.8 all-to-all-done.2.received
  87.4 0.7 copy-done.6
  88.1 3.8 %update.1 = (bf16[2,256,1792]{2,1,0:T(8,128)(2,1)}, f32[2,8,256]{2,1,0:T(8,128)}, f32[2,8,256]{2,1,0:T(8,128)}) custom-call(s32[6]{0:T(128)} %pad_add_fusion.place, bf16[64,8,384]{2,1,0:T(8,128)(2,1)} %copy-done.6, bf16[2,256,1792]{2,1,0:T(8,128)(2,1)} %get-tuple-element.12.proj, bf16[4,2,8,1792]{3,2,1,0:T(8,128)(2,1)} %copy-done.3, ...), custom_call_target="tpu_custom_call" | custom-call | tf_op jit(solution)/shard_map/update/pallas_call | solution.py:353
  (32 shorter events, 0.1 us)
Async XLA Ops:
  11.3 38.5 %copy-start.4 = (bf16[2,8,1792]{2,1,0:T(8,128)(2,1)S(1)}, bf16[2,8,1792]{2,1,0:T(8,128)(2,1)}, u32[]{:S(2)}) copy-start(bf16[2,8,1792]{2,1,0:T(8,128)(2,1)} %get-tuple-element.11.refs_0_) | copy-start | bytes 172036
  11.3 58.2 %copy-start.5 = (s32[6]{0:T(128)S(1)}, s32[6]{0:T(128)}, u32[]{:S(2)}) copy-start(s32[6]{0:T(128)} %pad_add_fusion.place) | copy-start | bytes 76
  11.3 24.5 %all-to-all-start = ((bf16[64,8,640]{2,1,0:T(8,128)(2,1)}), bf16[64,8,640]{2,1,0:T(8,128)(2,1)S(1)}, u32[]{:S(2)}, u32[]{:S(2)}) async-start(bf16[64,8,640]{2,1,0:T(8,128)(2,1)} %get-tuple-element.8), calls=%async_computation | async-start | bytes 1310720 | tf_op jit(solution)/shard_map/all_to_all | solution.py:315
  22.3 27.4 %collective-permute-start.3 = (bf16[2,8,1792]{2,1,0:T(8,128)(2,1)}, bf16[2,8,1792]{2,1,0:T(8,128)(2,1)S(1)}, u32[]{:S(2)}, u32[]{:S(2)}) collective-permute-start(bf16[2,8,1792]{2,1,0:T(8,128)(2,1)} %get-tuple-element.11.refs_0_), channel_id=1, source_target_pairs={{0,384},{16,400},{32,416},{48,432},{64,448},{80,464},{96,480},{112... | collective-permute-start | bytes 172040 | tf_op jit(solution)/shard_map/ppermute | solution.py:316
  27.3 22.4 %collective-permute-start.2 = (bf16[2,8,1792]{2,1,0:T(8,128)(2,1)}, bf16[2,8,1792]{2,1,0:T(8,128)(2,1)S(1)}, u32[]{:S(2)}, u32[]{:S(2)}) collective-permute-start(bf16[2,8,1792]{2,1,0:T(8,128)(2,1)} %get-tuple-element.11.refs_0_), channel_id=1, source_target_pairs={{0,256},{16,272},{32,288},{48,304},{64,320},{80,336},{96,352},{112... | collective-permute-start | bytes 172040 | tf_op jit(solution)/shard_map/ppermute | solution.py:316
  29.2 20.5 %collective-permute-start.1 = (bf16[2,8,1792]{2,1,0:T(8,128)(2,1)}, bf16[2,8,1792]{2,1,0:T(8,128)(2,1)S(1)}, u32[]{:S(2)}, u32[]{:S(2)}) collective-permute-start(bf16[2,8,1792]{2,1,0:T(8,128)(2,1)} %get-tuple-element.11.refs_0_), channel_id=1, source_target_pairs={{0,128},{16,144},{32,160},{48,176},{64,192},{80,208},{96,224},{112... | collective-permute-start | bytes 172040 | tf_op jit(solution)/shard_map/ppermute | solution.py:316
  36.5 33.0 %all-to-all-start.1 = ((bf16[8,8,512]{2,1,0:T(8,128)(2,1)}), bf16[8,8,512]{2,1,0:T(8,128)(2,1)S(1)}, u32[]{:S(2)}, u32[]{:S(2)}) async-start(bf16[8,8,512]{2,1,0:T(8,128)(2,1)} %get-tuple-element.9), calls=%async_computation.1 | async-start | bytes 131072 | tf_op jit(solution)/shard_map/all_to_all | solution.py:328
  49.8 37.6 %copy-start.3 = (bf16[4,2,8,1792]{3,2,1,0:T(8,128)(2,1)}, bf16[4,2,8,1792]{3,2,1,0:T(8,128)(2,1)S(1)}, u32[]{:S(2)}) copy-start(bf16[4,2,8,1792]{3,2,1,0:T(8,128)(2,1)S(1)} %join.1.refs_0_) | copy-start | bytes 688132
  49.8 19.7 %collective-permute-start.6 = (bf16[4,2,8,1792]{3,2,1,0:T(8,128)(2,1)S(1)}, bf16[4,2,8,1792]{3,2,1,0:T(8,128)(2,1)S(1)}, u32[]{:S(2)}, u32[]{:S(2)}) collective-permute-start(bf16[4,2,8,1792]{3,2,1,0:T(8,128)(2,1)S(1)} %join.1.refs_0_), channel_id=1, source_target_pairs={{0,96},{16,112},{32,64},{48,80},{64,32},{80,48},{96,0},{112,16},{1... | collective-permute-start | bytes 688136 | tf_op jit(solution)/shard_map/ppermute | solution.py:338
  52.5 17.0 %collective-permute-start.5 = (bf16[4,2,8,1792]{3,2,1,0:T(8,128)(2,1)S(1)}, bf16[4,2,8,1792]{3,2,1,0:T(8,128)(2,1)S(1)}, u32[]{:S(2)}, u32[]{:S(2)}) collective-permute-start(bf16[4,2,8,1792]{3,2,1,0:T(8,128)(2,1)S(1)} %join.1.refs_0_), channel_id=1, source_target_pairs={{0,64},{16,80},{32,96},{48,112},{64,0},{80,16},{96,32},{112,48},{1... | collective-permute-start | bytes 688136 | tf_op jit(solution)/shard_map/ppermute | solution.py:338
  55.6 13.9 %collective-permute-start.4 = (bf16[4,2,8,1792]{3,2,1,0:T(8,128)(2,1)S(1)}, bf16[4,2,8,1792]{3,2,1,0:T(8,128)(2,1)S(1)}, u32[]{:S(2)}, u32[]{:S(2)}) collective-permute-start(bf16[4,2,8,1792]{3,2,1,0:T(8,128)(2,1)S(1)} %join.1.refs_0_), channel_id=1, source_target_pairs={{0,32},{16,48},{32,0},{48,16},{64,96},{80,112},{96,64},{112,80},{1... | collective-permute-start | bytes 688136 | tf_op jit(solution)/shard_map/ppermute | solution.py:338
  58.8 10.7 %collective-permute-start = (bf16[2,128,256]{2,1,0:T(8,128)(2,1)S(1)}, bf16[2,128,256]{2,1,0:T(8,128)(2,1)S(1)}, u32[]{:S(2)}, u32[]{:S(2)}) collective-permute-start(bf16[2,128,256]{2,1,0:T(8,128)(2,1)S(1)} %get-tuple-element.10.refs_4_.near), channel_id=1, source_target_pairs={{0,256},{16,272},{32,288},{48,304},{64,320},{80,336},{96,352},{112... | collective-permute-start | bytes 393224 | tf_op jit(solution)/shard_map/ppermute | solution.py:329
  69.5 17.9 %copy-start = (bf16[4,2,8,1792]{3,2,1,0:T(8,128)(2,1)}, bf16[4,2,8,1792]{3,2,1,0:T(8,128)(2,1)S(1)}, u32[]{:S(2)}) copy-start(bf16[4,2,8,1792]{3,2,1,0:T(8,128)(2,1)S(1)} %collective-permute-done.6.refs_2_.refs_3_) | copy-start | bytes 688132
  69.5 17.9 %copy-start.1 = (bf16[4,2,8,1792]{3,2,1,0:T(8,128)(2,1)}, bf16[4,2,8,1792]{3,2,1,0:T(8,128)(2,1)S(1)}, u32[]{:S(2)}) copy-start(bf16[4,2,8,1792]{3,2,1,0:T(8,128)(2,1)S(1)} %collective-permute-done.5.refs_1_.refs_2_) | copy-start | bytes 688132
  69.5 17.9 %copy-start.2 = (bf16[4,2,8,1792]{3,2,1,0:T(8,128)(2,1)}, bf16[4,2,8,1792]{3,2,1,0:T(8,128)(2,1)S(1)}, u32[]{:S(2)}) copy-start(bf16[4,2,8,1792]{3,2,1,0:T(8,128)(2,1)S(1)} %collective-permute-done.4.refs_0_.refs_1_) | copy-start | bytes 688132
  71.5 15.9 %all-to-all-start.2 = ((bf16[64,8,384]{2,1,0:T(8,128)(2,1)}), bf16[64,8,384]{2,1,0:T(8,128)(2,1)S(1)}, u32[]{:S(2)}, u32[]{:S(2)}) async-start(bf16[64,8,384]{2,1,0:T(8,128)(2,1)} %moment.1), calls=%async_computation.2 | async-start | bytes 786432 | tf_op jit(solution)/shard_map/all_to_all | solution.py:347
  76.4 8.8 %collective-permute-start.7 = (bf16[4,2,8,1792]{3,2,1,0:T(8,128)(2,1)S(1)}, bf16[4,2,8,1792]{3,2,1,0:T(8,128)(2,1)S(1)}, u32[]{:S(2)}, u32[]{:S(2)}) collective-permute-start(bf16[4,2,8,1792]{3,2,1,0:T(8,128)(2,1)S(1)} %join.1.refs_0_), channel_id=1, source_target_pairs={{0,16},{16,0},{32,48},{48,32},{64,80},{80,64},{96,112},{112,96},{1... | collective-permute-start | bytes 688136 | tf_op jit(solution)/shard_map/ppermute | solution.py:348
  78.8 6.3 %collective-permute-start.10 = (bf16[4,2,8,1792]{3,2,1,0:T(8,128)(2,1)S(1)}, bf16[4,2,8,1792]{3,2,1,0:T(8,128)(2,1)S(1)}, u32[]{:S(2)}, u32[]{:S(2)}) collective-permute-start(bf16[4,2,8,1792]{3,2,1,0:T(8,128)(2,1)S(1)} %collective-permute-done.6.refs_2_.refs_3_), channel_id=1, source_target_pairs={{0,16},{16,0},{32,48},{48,32},{64,80},{80,64},{96,112},{112,96},{1... | collective-permute-start | bytes 688136 | tf_op jit(solution)/shard_map/ppermute | solution.py:348
  80.8 4.4 %collective-permute-start.9 = (bf16[4,2,8,1792]{3,2,1,0:T(8,128)(2,1)S(1)}, bf16[4,2,8,1792]{3,2,1,0:T(8,128)(2,1)S(1)}, u32[]{:S(2)}, u32[]{:S(2)}) collective-permute-start(bf16[4,2,8,1792]{3,2,1,0:T(8,128)(2,1)S(1)} %collective-permute-done.5.refs_1_.refs_2_), channel_id=1, source_target_pairs={{0,16},{16,0},{32,48},{48,32},{64,80},{80,64},{96,112},{112,96},{1... | collective-permute-start | bytes 688136 | tf_op jit(solution)/shard_map/ppermute | solution.py:348
  83.2 3.4 %collective-permute-start.8 = (bf16[4,2,8,1792]{3,2,1,0:T(8,128)(2,1)S(1)}, bf16[4,2,8,1792]{3,2,1,0:T(8,128)(2,1)S(1)}, u32[]{:S(2)}, u32[]{:S(2)}) collective-permute-start(bf16[4,2,8,1792]{3,2,1,0:T(8,128)(2,1)S(1)} %collective-permute-done.4.refs_0_.refs_1_), channel_id=1, source_target_pairs={{0,16},{16,0},{32,48},{48,32},{64,80},{80,64},{96,112},{112,96},{1... | collective-permute-start | bytes 688136 | tf_op jit(solution)/shard_map/ppermute | solution.py:348
  85.1 2.3 %copy-start.7 = (bf16[4,2,8,1792]{3,2,1,0:T(8,128)(2,1)}, bf16[4,2,8,1792]{3,2,1,0:T(8,128)(2,1)S(1)}, u32[]{:S(2)}) copy-start(bf16[4,2,8,1792]{3,2,1,0:T(8,128)(2,1)S(1)} %collective-permute-done.7.refs_4_) | copy-start | bytes 688132
  85.1 2.3 %copy-start.8 = (bf16[4,2,8,1792]{3,2,1,0:T(8,128)(2,1)}, bf16[4,2,8,1792]{3,2,1,0:T(8,128)(2,1)S(1)}, u32[]{:S(2)}) copy-start(bf16[4,2,8,1792]{3,2,1,0:T(8,128)(2,1)S(1)} %collective-permute-done.10.refs_7_) | copy-start | bytes 688132
  85.2 2.3 %copy-start.9 = (bf16[4,2,8,1792]{3,2,1,0:T(8,128)(2,1)}, bf16[4,2,8,1792]{3,2,1,0:T(8,128)(2,1)S(1)}, u32[]{:S(2)}) copy-start(bf16[4,2,8,1792]{3,2,1,0:T(8,128)(2,1)S(1)} %collective-permute-done.9.refs_6_) | copy-start | bytes 688132
  86.6 0.9 copy-start.10
  (1 other events, 0.7 us)

commit v3 on v2

--- a/solution.py
+++ b/solution.py
@@ -85,98 +85,107 @@
 
 
 def project_kernel(
-    place,
+    seeds,
+    old_seeds,
     grads_hbm,
-    first_moment,
-    second_moment,
-    weights,
+    first_hbm,
+    second_hbm,
+    weights_hbm,
     proj_hbm,
     send,
     weights_out,
     grads,
+    moments,
     proj,
     keys,
+    keys_later,
     columns2,
     old_rows,
-    load_sems,
-    store_sems,
+    grads_sems,
+    moment_sems,
+    weights_sem,
+    proj_sems,
     *,
     spread,
 ):
     layers, rank, cols = proj.shape
-    dp, mp = place[0], place[1]
+    dp, mp = lax.axis_index("dp"), lax.axis_index("mp")
     tiles = cols // 128
     share = 64 // layers
-    loads = [
-        pltpu.make_async_copy(grads_hbm.at[0, layer], grads.at[layer], load_sems.at[layer])
+    grads_in = [
+        pltpu.make_async_copy(grads_hbm.at[0, layer], grads.at[layer], grads_sems.at[layer])
         for layer in range(layers)
     ]
-    stores = [
-        pltpu.make_async_copy(proj.at[layer], proj_hbm.at[layer], store_sems.at[layer])
+    moments_in = [
+        pltpu.make_async_copy(source, moments.at[which], moment_sems.at[which])
+        for which, source in enumerate((first_hbm, second_hbm))
+    ]
+    weights_move = pltpu.make_async_copy(weights_hbm, weights_out, weights_sem)
+    proj_out = [
+        pltpu.make_async_copy(proj.at[layer], proj_hbm.at[layer], proj_sems.at[layer])
         for layer in range(layers)
     ]
-    for load in loads:
-        load.start()
-    weights_out[...] = weights[...]
+    for copy in (*grads_in, *moments_in, weights_move):
+        copy.start()
+
+    def both_halves(eight):
+        return jnp.concatenate([eight, eight], axis=0)
+
     lanes = lax.broadcasted_iota(jnp.int32, (8, cols), 1) + mp * cols
     row = lax.broadcasted_iota(jnp.int32, (rank, 128), 0)
-
-    def both_halves(eight):
-        return jnp.concatenate([eight, eight], axis=0)
-
+    old_block = dp % (rank // 16)
+    old_row = lax.broadcasted_iota(jnp.int32, (16, 128), 0) + old_block * 16
+    for layer in range(layers):
+        offset = lax.rem(old_seeds[layer], PRIME)
+        mine = row_keys(offset, old_row)
+        later = below(mine + 3 * 12345, PRIME)
+        old_columns2 = column_keys(offset, lanes)
+        for tile in range(tiles):
+            cut = slice(tile * 128, tile * 128 + 128)
+            old_rows[layer, :, cut] = entries(
+                mine, later, both_halves(old_columns2[:, cut]), spread
+            )
+        offset = lax.rem(seeds[layer], PRIME)
+        keys[layer] = row_keys(offset, row)
+        keys_later[layer] = below(keys[layer] + 3 * 12345, PRIME)
+        columns2[layer] = column_keys(offset, lanes)
+
+    for layer in range(layers):
+
+        def chunk(index, _, layer=layer):
+            rows = pl.ds(pl.multiple_of(index * 16, 16), 16)
+            mine, later = keys[layer, rows, :], keys_later[layer, rows, :]
+            for tile in range(tiles):
+                cut = slice(tile * 128, tile * 128 + 128)
+                proj[layer, rows, cut] = entries(
+                    mine, later, both_halves(columns2[layer, :, cut]), spread
+                )
+            return 0
+
+        lax.fori_loop(0, rank // 16, chunk, 0, unroll=2)
+        proj_out[layer].start()
+
+    for copy in (*grads_in, *moments_in):
+        copy.wait()
     y = mp % 4
+    spot_row = lax.broadcasted_iota(jnp.int32, (16, rank), 0) + old_block * 16
+    spot_lane = lax.broadcasted_iota(jnp.int32, (16, rank), 1)
     for layer in range(layers):
         group = slice(share * layer, share * layer + share)
-        offset = lax.rem(place[2 + layer], PRIME)
-        keys[...] = row_keys(offset, row)
-        columns2[...] = column_keys(offset, lanes)
-
-        def chunk(index, _, layer=layer):
-            at = pl.multiple_of(index * 16, 16)
-            mine = keys[pl.ds(at, 16), :]
-            later = below(mine + 3 * 12345, PRIME)
-            for tile in range(tiles):
-                cut = slice(tile * 128, tile * 128 + 128)
-                proj[layer, pl.ds(at, 16), cut] = entries(
-                    mine, later, both_halves(columns2[:, cut]), spread
-                )
-            return 0
-
-        lax.fori_loop(0, rank // 16, chunk, 0)
-        stores[layer].start()
-        loads[layer].wait()
         compressed = lax.dot_general(proj[layer], grads[layer], NT, preferred_element_type=F32)
         send[group, :, 0:rank] = compressed.reshape(share, 8, rank).astype(BF16)
-        moments = jnp.where(y < 2, first_moment[layer], second_moment[layer])
-        half = jnp.where(y % 2 == 0, moments[:, 0:128], moments[:, 128:256])
+        gram = lax.dot_general(proj[layer], old_rows[layer], NT, preferred_element_type=F32)
+        mine_layer = dp // (rank // 16) == layer
+        spot = jnp.where((spot_row == spot_lane) & mine_layer, 1.0, 0.0).astype(BF16)
+        placed = jnp.dot(gram.astype(BF16), spot, preferred_element_type=F32)
+        send[group, :, rank : 2 * rank] = placed.reshape(share, 8, rank).astype(BF16)
+        moment = jnp.where(y < 2, moments[0, layer], moments[1, layer])
+        half = jnp.where(y % 2 == 0, moment[:, 0:128], moment[:, 128:256])
         send[group, :, 2 * rank : 2 * rank + 128] = jnp.broadcast_to(
             half[None], (share, 8, 128)
         ).astype(BF16)
-
-        mine_layer = dp // (rank // 16)
-
-        @pl.when(mine_layer == layer)
-        def _(layer=layer, group=group):
-            old_rows[...] = jnp.zeros_like(old_rows)
-            old_offset = lax.rem(place[4 + layer], PRIME)
-            at = pl.multiple_of((dp % (rank // 16)) * 16, 16)
-            mine = row_keys(old_offset, lax.broadcasted_iota(jnp.int32, (16, 128), 0) + at)
-            later = below(mine + 3 * 12345, PRIME)
-            columns2[...] = column_keys(old_offset, lanes)
-            for tile in range(tiles):
-                cut = slice(tile * 128, tile * 128 + 128)
-                old_rows[pl.ds(at, 16), cut] = entries(
-                    mine, later, both_halves(columns2[:, cut]), spread
-                )
-            gram = lax.dot_general(proj[layer], old_rows[...], NT, preferred_element_type=F32)
-            send[group, :, rank : 2 * rank] = gram.reshape(share, 8, rank).astype(BF16)
-
-        @pl.when(mine_layer != layer)
-        def _(group=group):
-            send[group, :, rank : 2 * rank] = jnp.zeros((share, 8, rank), BF16)
-
-    for store in stores:
-        store.wait()
+    for copy in (weights_move, *proj_out):
+        copy.wait()
 
 
 def summed(received, width):
@@ -203,11 +212,11 @@
         joined[slot] = piece[...]
 
 
-def moment_kernel(place, received, near, far, *refs):
+def moment_kernel(received, near, far, *refs):
     send = refs[-1]
     total = summed(received, 512)
     compressed, gram = total[:, 0:256], total[:, 256:512]
-    upper = (place[0] // 16) == 1
+    upper = (lax.axis_index("dp") // 16) == 1
 
     def times(left, which):
         near_part, far_part = near[which].astype(F32), far[which].astype(F32)
@@ -242,12 +251,11 @@
         ).astype(BF16)
 
 
-def update_kernel(place, received, proj, *refs):
+def update_kernel(received, proj, *refs):
     own, other = refs[0:4], refs[4:8]
     new_weights, new_first, new_second, update = refs[8:]
-    dp = place[0]
+    dp = lax.axis_index("dp")
     z, x, core = dp // 8, dp // 2 % 4, dp % 2
-    cols = proj.shape[2]
     direction = received[:, :, 0:256].astype(F32).reshape(256, 256).astype(BF16)
     update[...] = 0.5 * lax.dot_general(direction, proj[0], TN, preferred_element_type=F32)
     for x_bits in FOUR:
@@ -277,20 +285,17 @@
     layers, block, cols = weights.shape
     rank = first_moment.shape[2]
     spread = math.sqrt(12.0 / rank)
-    place = jnp.concatenate(
-        [jnp.stack([lax.axis_index("dp"), lax.axis_index("mp")]).astype(jnp.int32), new_seeds, old_seeds]
-    )
     smem = pl.BlockSpec(memory_space=pltpu.SMEM)
     vmem = pl.BlockSpec(memory_space=pltpu.VMEM)
     hbm = pl.BlockSpec(memory_space=pltpu.HBM)
     anywhere = pl.BlockSpec(memory_space=pl.ANY)
-    roomy = pltpu.CompilerParams(vmem_limit_bytes=56 * 2**20)
+    roomy = pltpu.CompilerParams(vmem_limit_bytes=251 * 2**18)
     small = pltpu.CompilerParams(vmem_limit_bytes=8 * 2**20)
 
     proj, send, weights = pl.pallas_call(
         functools.partial(project_kernel, spread=spread),
-        in_specs=[smem, hbm, vmem, vmem, vmem],
-        out_specs=[hbm, vmem, vmem],
+        in_specs=[smem, smem, hbm, hbm, hbm, hbm],
+        out_specs=[hbm, vmem, hbm],
         out_shape=[
             jax.ShapeDtypeStruct((layers, rank, cols), BF16),
             jax.ShapeDtypeStruct((64, 8, 640), BF16),
@@ -298,11 +303,15 @@
         ],
         scratch_shapes=[
             pltpu.VMEM((layers, rank, cols), BF16),
+            pltpu.VMEM((2, layers, block, rank), F32),
             pltpu.VMEM((layers, rank, cols), BF16),
-            pltpu.VMEM((rank, 128), jnp.int32),
-            pltpu.VMEM((8, cols), jnp.int32),
-            pltpu.VMEM((rank, cols), BF16),
+            pltpu.VMEM((layers, rank, 128), jnp.int32),
+            pltpu.VMEM((layers, rank, 128), jnp.int32),
+            pltpu.VMEM((layers, 8, cols), jnp.int32),
+            pltpu.VMEM((layers, 16, cols), BF16),
             pltpu.SemaphoreType.DMA((layers,)),
+            pltpu.SemaphoreType.DMA((2,)),
+            pltpu.SemaphoreType.DMA(()),
             pltpu.SemaphoreType.DMA((layers,)),
         ],
         compiler_params=roomy,
@@ -310,7 +319,7 @@
             flops=8 * 10**9, bytes_accessed=6 * 10**6, transcendentals=0
         ),
         name="project",
-    )(place, grads, first_moment, second_moment, weights)
+    )(new_seeds, old_seeds, grads, first_moment, second_moment, weights)
 
     received = lax.all_to_all(send, BOTH, 0, 0, axis_index_groups=SLABS, tiled=True)
     column = [weights] + [lax.ppermute(weights, "dp", swap(bits, 0, 0)) for bits in (1, 2, 3)]
@@ -338,12 +347,12 @@
     own = [column] + [lax.ppermute(column, "dp", swap(0, bits, 0)) for bits in (1, 2, 3)]
     send = pl.pallas_call(
         moment_kernel,
-        in_specs=[smem, vmem, vmem, vmem] + [anywhere] * 3,
+        in_specs=[vmem, vmem, vmem] + [anywhere] * 3,
         out_specs=vmem,
         out_shape=jax.ShapeDtypeStruct((64, 8, 384), BF16),
         compiler_params=small,
         name="moment",
-    )(place, received, near, far, *own[1:])
+    )(received, near, far, *own[1:])
     received = lax.all_to_all(send, BOTH, 0, 0, axis_index_groups=SLABS, tiled=True)
     other = [lax.ppermute(piece, "dp", swap(0, 0, 1)) for piece in own]
 
@@ -354,7 +363,6 @@
         update_kernel,
         grid=(layers,),
         in_specs=[
-            smem,
             pl.BlockSpec((64 // layers, 8, 384), lambda layer: (layer, 0, 0)),
             whole,
         ]
@@ -366,9 +374,9 @@
             jax.ShapeDtypeStruct((layers, block, rank), F32),
         ],
         scratch_shapes=[pltpu.VMEM((rank, cols), F32)],
-        compiler_params=pltpu.CompilerParams(vmem_limit_bytes=56 * 2**20),
+        compiler_params=roomy,
         name="update",
-    )(place, received, proj, *own, *other)
+    )(received, proj, *own, *other)
 
 
 def solution(mesh):

time: 92.7 us -> 90 us (0.971)
  waiting for transfers between devices: 12.8 us -> 11 us
  Pallas kernels: 15.8 us -> 14.4 us
  other arithmetic: 1.33 us -> 0 us
  starting transfers between devices: 60.3 us -> 61.6 us
    concatenate x1 -> x0, other arithmetic: 1.33 us -> none  [shards(): jnp.concatenate([jnp.stack([lax.axis_index('dp'), lax.axis_index('mp')])....]
    ppermute x4, waiting for transfers between devices: 1.4 us -> 0.15 us  [shards(): other = [lax.ppermute(piece, 'dp', swap(0, 0, 1)) for piece in own]]
where the time goes in v3:
time: 90 us; the launch traced here: 89.3 us
  starting transfers between devices  61.6 us (68%)
  Pallas kernels  14.4 us (16%)
  waiting for transfers between devices  11 us (12%)
  local copies, waits for them, and re-layouts  1.42 us (2%)
    all_to_all x2, starting transfers between devices, shards(): lax.all_to_all(send, BOTH, 0, 0, axis_index_groups=SLABS, tiled=True)  16.7 us
    all_to_all x1, starting transfers between devices, shards(): lax.all_to_all(send, BOTH, 0, 0, axis_index_groups=LINES, tiled=True)  13.2 us
    ppermute x3, starting transfers between devices, shards(): lax.ppermute(weights, 'dp', swap(bits, 0, 0))  9.6 us
    ppermute x3, starting transfers between devices, shards(): lax.ppermute(column, 'dp', swap(0, bits, 0))  8.98 us
    ppermute x4, starting transfers between devices, shards(): other = [lax.ppermute(piece, 'dp', swap(0, 0, 1)) for piece in own]  8.79 us
    pallas_call x1, Pallas kernels, shards(): pl.pallas_call(functools.partial(project_kernel, spread=spread), in_specs...  8.49 us
    ppermute x1, waiting for transfers between devices, shards(): far = lax.ppermute(near, 'dp', swap(2, 0, 0))  6.42 us
    all_to_all x2, waiting for transfers between devices, shards(): lax.all_to_all(send, BOTH, 0, 0, axis_index_groups=SLABS, tiled=True)  4.42 us
  transfers between devices with their start and end apart: 14, of which 4 were waited for; matrix products, arithmetic and copies ran while one was open for 0% of the time, Pallas kernels for 1%

profile of v3, /device:TPU:1, one launch (start us, length us, event | category | flops | bytes accessed | tf_op | source)
XLA Modules:
  0.0 89.3 jit_solution(6092367337820768953)
XLA Ops:
  0.6 8.5 %project.1 = (bf16[2,256,1792]{2,1,0:T(8,128)(2,1)}, bf16[64,8,640]{2,1,0:T(8,128)(2,1)}, bf16[2,8,1792]{2,1,0:T(8,128)(2,1)}) custom-call(s32[2]{0:T(128)} %seeds.1, s32[2]{0:T(128)} %old_seeds.1, bf16[1,2,256,1792]{3,2,1,0:T(8,128)(2,1)} %grads_hbm.1, f32[2,8,256]{2,1,0:T(8,128)} %first_hbm.1, f32[2,8,256]{2,1,0:T(8,128)} %second_hbm.1, ...), custom_call_target="tpu_custom_call" | custom-call | flops 8000000000 | bytes 6000000 | tf_op jit(solution)/shard_map/project/pallas_call | solution.py:295
  9.1 11.1 %all-to-all-start = ((bf16[64,8,640]{2,1,0:T(8,128)(2,1)}), bf16[64,8,640]{2,1,0:T(8,128)(2,1)S(1)}, u32[]{:S(2)}, u32[]{:S(2)}) async-start(bf16[64,8,640]{2,1,0:T(8,128)(2,1)} %get-tuple-element.8), calls=%async_computation | async-start | bytes 1310720 | tf_op jit(solution)/shard_map/all_to_all | solution.py:324
  20.2 5.5 %collective-permute-start.3 = (bf16[2,8,1792]{2,1,0:T(8,128)(2,1)}, bf16[2,8,1792]{2,1,0:T(8,128)(2,1)S(1)}, u32[]{:S(2)}, u32[]{:S(2)}) collective-permute-start(bf16[2,8,1792]{2,1,0:T(8,128)(2,1)} %get-tuple-element.11.refs_0_), channel_id=1, source_target_pairs={{0,384},{16,400},{32,416},{48,432},{64,448},{80,464},{96,480},{112... | collective-permute-start | bytes 172040 | tf_op jit(solution)/shard_map/ppermute | solution.py:325
  25.7 1.9 %collective-permute-start.2 = (bf16[2,8,1792]{2,1,0:T(8,128)(2,1)}, bf16[2,8,1792]{2,1,0:T(8,128)(2,1)S(1)}, u32[]{:S(2)}, u32[]{:S(2)}) collective-permute-start(bf16[2,8,1792]{2,1,0:T(8,128)(2,1)} %get-tuple-element.11.refs_0_), channel_id=1, source_target_pairs={{0,256},{16,272},{32,288},{48,304},{64,320},{80,336},{96,352},{112... | collective-permute-start | bytes 172040 | tf_op jit(solution)/shard_map/ppermute | solution.py:325
  27.7 2.2 %collective-permute-start.1 = (bf16[2,8,1792]{2,1,0:T(8,128)(2,1)}, bf16[2,8,1792]{2,1,0:T(8,128)(2,1)S(1)}, u32[]{:S(2)}, u32[]{:S(2)}) collective-permute-start(bf16[2,8,1792]{2,1,0:T(8,128)(2,1)} %get-tuple-element.11.refs_0_), channel_id=1, source_target_pairs={{0,128},{16,144},{32,160},{48,176},{64,192},{80,208},{96,224},{112... | collective-permute-start | bytes 172040 | tf_op jit(solution)/shard_map/ppermute | solution.py:325
  29.9 3.9 %all-to-all-done.received = bf16[64,8,640]{2,1,0:T(8,128)(2,1)S(1)} async-done(((bf16[64,8,640]{2,1,0:T(8,128)(2,1)}), bf16[64,8,640]{2,1,0:T(8,128)(2,1)S(1)}, u32[]{:S(2)}, u32[]{:S(2)}) %all-to-all-start) | async-done | bytes 655392 | tf_op jit(solution)/shard_map/all_to_all | solution.py:324
  33.7 0.7 slab_sum.1
  34.5 13.2 %all-to-all-start.1 = ((bf16[8,8,512]{2,1,0:T(8,128)(2,1)}), bf16[8,8,512]{2,1,0:T(8,128)(2,1)S(1)}, u32[]{:S(2)}, u32[]{:S(2)}) async-start(bf16[8,8,512]{2,1,0:T(8,128)(2,1)} %get-tuple-element.9), calls=%async_computation.1 | async-start | bytes 131072 | tf_op jit(solution)/shard_map/all_to_all | solution.py:337
  47.7 2.7 %collective-permute-start.6 = (bf16[4,2,8,1792]{3,2,1,0:T(8,128)(2,1)S(1)}, bf16[4,2,8,1792]{3,2,1,0:T(8,128)(2,1)S(1)}, u32[]{:S(2)}, u32[]{:S(2)}) collective-permute-start(bf16[4,2,8,1792]{3,2,1,0:T(8,128)(2,1)S(1)} %join.1.refs_0_), channel_id=1, source_target_pairs={{0,96},{16,112},{32,64},{48,80},{64,32},{80,48},{96,0},{112,16},{1... | collective-permute-start | bytes 688136 | tf_op jit(solution)/shard_map/ppermute | solution.py:347
  50.4 3.1 %collective-permute-start.5 = (bf16[4,2,8,1792]{3,2,1,0:T(8,128)(2,1)S(1)}, bf16[4,2,8,1792]{3,2,1,0:T(8,128)(2,1)S(1)}, u32[]{:S(2)}, u32[]{:S(2)}) collective-permute-start(bf16[4,2,8,1792]{3,2,1,0:T(8,128)(2,1)S(1)} %join.1.refs_0_), channel_id=1, source_target_pairs={{0,64},{16,80},{32,96},{48,112},{64,0},{80,16},{96,32},{112,48},{1... | collective-permute-start | bytes 688136 | tf_op jit(solution)/shard_map/ppermute | solution.py:347
  53.6 3.2 %collective-permute-start.4 = (bf16[4,2,8,1792]{3,2,1,0:T(8,128)(2,1)S(1)}, bf16[4,2,8,1792]{3,2,1,0:T(8,128)(2,1)S(1)}, u32[]{:S(2)}, u32[]{:S(2)}) collective-permute-start(bf16[4,2,8,1792]{3,2,1,0:T(8,128)(2,1)S(1)} %join.1.refs_0_), channel_id=1, source_target_pairs={{0,32},{16,48},{32,0},{48,16},{64,96},{80,112},{96,64},{112,80},{1... | collective-permute-start | bytes 688136 | tf_op jit(solution)/shard_map/ppermute | solution.py:347
  56.7 4.3 %collective-permute-start = (bf16[2,128,256]{2,1,0:T(8,128)(2,1)S(1)}, bf16[2,128,256]{2,1,0:T(8,128)(2,1)S(1)}, u32[]{:S(2)}, u32[]{:S(2)}) collective-permute-start(bf16[2,128,256]{2,1,0:T(8,128)(2,1)S(1)} %get-tuple-element.10.refs_4_.near), channel_id=1, source_target_pairs={{0,256},{16,272},{32,288},{48,304},{64,320},{80,336},{96,352},{112... | collective-permute-start | bytes 393224 | tf_op jit(solution)/shard_map/ppermute | solution.py:338
  61.0 6.4 %collective-permute-done.far = bf16[2,128,256]{2,1,0:T(8,128)(2,1)S(1)} collective-permute-done((bf16[2,128,256]{2,1,0:T(8,128)(2,1)S(1)}, bf16[2,128,256]{2,1,0:T(8,128)(2,1)S(1)}, u32[]{:S(2)}, u32[]{:S(2)}) %collective-permute-start) | collective-permute-done | bytes 131104 | tf_op jit(solution)/shard_map/ppermute | solution.py:338
  67.5 1.4 %moment.1 = bf16[64,8,384]{2,1,0:T(8,128)(2,1)} custom-call(bf16[8,8,512]{2,1,0:T(8,128)(2,1)S(1)} %all-to-all-done.1.received, bf16[2,128,256]{2,1,0:T(8,128)(2,1)S(1)} %get-tuple-element.10.refs_4_.near, bf16[2,128,256]{2,1,0:T(8,128)(2,1)S(1)} %collective-permute-done.far, bf16[4,2,8,1792]{3,2,1,0:T(8,128)(2,1)S(1)} %collective-permute-done.4.refs_0_.refs_1_, ...), custom_call_target="tpu_custom_call" | custom-call | tf_op jit(solution)/shard_map/moment/pallas_call | solution.py:348
  68.9 5.6 %all-to-all-start.2 = ((bf16[64,8,384]{2,1,0:T(8,128)(2,1)}), bf16[64,8,384]{2,1,0:T(8,128)(2,1)}, u32[]{:S(2)}, u32[]{:S(2)}) async-start(bf16[64,8,384]{2,1,0:T(8,128)(2,1)} %moment.1), calls=%async_computation.2 | async-start | bytes 786432 | tf_op jit(solution)/shard_map/all_to_all | solution.py:356
  74.5 2.5 %collective-permute-start.7 = (bf16[4,2,8,1792]{3,2,1,0:T(8,128)(2,1)S(1)}, bf16[4,2,8,1792]{3,2,1,0:T(8,128)(2,1)S(1)}, u32[]{:S(2)}, u32[]{:S(2)}) collective-permute-start(bf16[4,2,8,1792]{3,2,1,0:T(8,128)(2,1)S(1)} %join.1.refs_0_), channel_id=1, source_target_pairs={{0,16},{16,0},{32,48},{48,32},{64,80},{80,64},{96,112},{112,96},{1... | collective-permute-start | bytes 688136 | tf_op jit(solution)/shard_map/ppermute | solution.py:357
  77.1 1.9 %collective-permute-start.10 = (bf16[4,2,8,1792]{3,2,1,0:T(8,128)(2,1)S(1)}, bf16[4,2,8,1792]{3,2,1,0:T(8,128)(2,1)S(1)}, u32[]{:S(2)}, u32[]{:S(2)}) collective-permute-start(bf16[4,2,8,1792]{3,2,1,0:T(8,128)(2,1)S(1)} %collective-permute-done.6.refs_2_.refs_3_), channel_id=1, source_target_pairs={{0,16},{16,0},{32,48},{48,32},{64,80},{80,64},{96,112},{112,96},{1... | collective-permute-start | bytes 688136 | tf_op jit(solution)/shard_map/ppermute | solution.py:357
  79.0 2.4 %collective-permute-start.9 = (bf16[4,2,8,1792]{3,2,1,0:T(8,128)(2,1)S(1)}, bf16[4,2,8,1792]{3,2,1,0:T(8,128)(2,1)S(1)}, u32[]{:S(2)}, u32[]{:S(2)}) collective-permute-start(bf16[4,2,8,1792]{3,2,1,0:T(8,128)(2,1)S(1)} %collective-permute-done.5.refs_1_.refs_2_), channel_id=1, source_target_pairs={{0,16},{16,0},{32,48},{48,32},{64,80},{80,64},{96,112},{112,96},{1... | collective-permute-start | bytes 688136 | tf_op jit(solution)/shard_map/ppermute | solution.py:357
  81.4 1.9 %collective-permute-start.8 = (bf16[4,2,8,1792]{3,2,1,0:T(8,128)(2,1)S(1)}, bf16[4,2,8,1792]{3,2,1,0:T(8,128)(2,1)}, u32[]{:S(2)}, u32[]{:S(2)}) collective-permute-start(bf16[4,2,8,1792]{3,2,1,0:T(8,128)(2,1)S(1)} %collective-permute-done.4.refs_0_.refs_1_), channel_id=1, source_target_pairs={{0,16},{16,0},{32,48},{48,32},{64,80},{80,64},{96,112},{112,96},{1... | collective-permute-start | bytes 688136 | tf_op jit(solution)/shard_map/ppermute | solution.py:357
  83.4 0.7 copy-done.6
  84.1 0.7 copy-done.7
  84.8 0.1 collective-permute-done.8.refs_5_
  84.9 0.6 all-to-all-done.2.received
  85.5 3.8 %update.1 = (bf16[2,256,1792]{2,1,0:T(8,128)(2,1)}, f32[2,8,256]{2,1,0:T(8,128)}, f32[2,8,256]{2,1,0:T(8,128)}) custom-call(bf16[64,8,384]{2,1,0:T(8,128)(2,1)} %all-to-all-done.2.received, bf16[2,256,1792]{2,1,0:T(8,128)(2,1)} %get-tuple-element.12.proj, bf16[4,2,8,1792]{3,2,1,0:T(8,128)(2,1)} %copy-done, bf16[4,2,8,1792]{3,2,1,0:T(8,128)(2,1)} %copy-done.3, ...), custom_call_target="tpu_custom_call" | custom-call | tf_op jit(solution)/shard_map/update/pallas_call | solution.py:362
  (25 shorter events, 0.1 us)
Async XLA Ops:
  9.1 38.6 %copy-start.4 = (bf16[2,8,1792]{2,1,0:T(8,128)(2,1)S(1)}, bf16[2,8,1792]{2,1,0:T(8,128)(2,1)}, u32[]{:S(2)}) copy-start(bf16[2,8,1792]{2,1,0:T(8,128)(2,1)} %get-tuple-element.11.refs_0_) | copy-start | bytes 172036
  9.1 24.6 %all-to-all-start = ((bf16[64,8,640]{2,1,0:T(8,128)(2,1)}), bf16[64,8,640]{2,1,0:T(8,128)(2,1)S(1)}, u32[]{:S(2)}, u32[]{:S(2)}) async-start(bf16[64,8,640]{2,1,0:T(8,128)(2,1)} %get-tuple-element.8), calls=%async_computation | async-start | bytes 1310720 | tf_op jit(solution)/shard_map/all_to_all | solution.py:324
  20.2 27.4 %collective-permute-start.3 = (bf16[2,8,1792]{2,1,0:T(8,128)(2,1)}, bf16[2,8,1792]{2,1,0:T(8,128)(2,1)S(1)}, u32[]{:S(2)}, u32[]{:S(2)}) collective-permute-start(bf16[2,8,1792]{2,1,0:T(8,128)(2,1)} %get-tuple-element.11.refs_0_), channel_id=1, source_target_pairs={{0,384},{16,400},{32,416},{48,432},{64,448},{80,464},{96,480},{112... | collective-permute-start | bytes 172040 | tf_op jit(solution)/shard_map/ppermute | solution.py:325
  25.7 21.9 %collective-permute-start.2 = (bf16[2,8,1792]{2,1,0:T(8,128)(2,1)}, bf16[2,8,1792]{2,1,0:T(8,128)(2,1)S(1)}, u32[]{:S(2)}, u32[]{:S(2)}) collective-permute-start(bf16[2,8,1792]{2,1,0:T(8,128)(2,1)} %get-tuple-element.11.refs_0_), channel_id=1, source_target_pairs={{0,256},{16,272},{32,288},{48,304},{64,320},{80,336},{96,352},{112... | collective-permute-start | bytes 172040 | tf_op jit(solution)/shard_map/ppermute | solution.py:325
  27.7 20.0 %collective-permute-start.1 = (bf16[2,8,1792]{2,1,0:T(8,128)(2,1)}, bf16[2,8,1792]{2,1,0:T(8,128)(2,1)S(1)}, u32[]{:S(2)}, u32[]{:S(2)}) collective-permute-start(bf16[2,8,1792]{2,1,0:T(8,128)(2,1)} %get-tuple-element.11.refs_0_), channel_id=1, source_target_pairs={{0,128},{16,144},{32,160},{48,176},{64,192},{80,208},{96,224},{112... | collective-permute-start | bytes 172040 | tf_op jit(solution)/shard_map/ppermute | solution.py:325
  34.5 33.0 %all-to-all-start.1 = ((bf16[8,8,512]{2,1,0:T(8,128)(2,1)}), bf16[8,8,512]{2,1,0:T(8,128)(2,1)S(1)}, u32[]{:S(2)}, u32[]{:S(2)}) async-start(bf16[8,8,512]{2,1,0:T(8,128)(2,1)} %get-tuple-element.9), calls=%async_computation.1 | async-start | bytes 131072 | tf_op jit(solution)/shard_map/all_to_all | solution.py:337
  47.7 37.8 %copy-start = (bf16[4,2,8,1792]{3,2,1,0:T(8,128)(2,1)}, bf16[4,2,8,1792]{3,2,1,0:T(8,128)(2,1)S(1)}, u32[]{:S(2)}) copy-start(bf16[4,2,8,1792]{3,2,1,0:T(8,128)(2,1)S(1)} %join.1.refs_0_) | copy-start | bytes 688132
  47.7 19.7 %collective-permute-start.6 = (bf16[4,2,8,1792]{3,2,1,0:T(8,128)(2,1)S(1)}, bf16[4,2,8,1792]{3,2,1,0:T(8,128)(2,1)S(1)}, u32[]{:S(2)}, u32[]{:S(2)}) collective-permute-start(bf16[4,2,8,1792]{3,2,1,0:T(8,128)(2,1)S(1)} %join.1.refs_0_), channel_id=1, source_target_pairs={{0,96},{16,112},{32,64},{48,80},{64,32},{80,48},{96,0},{112,16},{1... | collective-permute-start | bytes 688136 | tf_op jit(solution)/shard_map/ppermute | solution.py:347
  50.4 17.0 %collective-permute-start.5 = (bf16[4,2,8,1792]{3,2,1,0:T(8,128)(2,1)S(1)}, bf16[4,2,8,1792]{3,2,1,0:T(8,128)(2,1)S(1)}, u32[]{:S(2)}, u32[]{:S(2)}) collective-permute-start(bf16[4,2,8,1792]{3,2,1,0:T(8,128)(2,1)S(1)} %join.1.refs_0_), channel_id=1, source_target_pairs={{0,64},{16,80},{32,96},{48,112},{64,0},{80,16},{96,32},{112,48},{1... | collective-permute-start | bytes 688136 | tf_op jit(solution)/shard_map/ppermute | solution.py:347
  53.6 13.9 %collective-permute-start.4 = (bf16[4,2,8,1792]{3,2,1,0:T(8,128)(2,1)S(1)}, bf16[4,2,8,1792]{3,2,1,0:T(8,128)(2,1)S(1)}, u32[]{:S(2)}, u32[]{:S(2)}) collective-permute-start(bf16[4,2,8,1792]{3,2,1,0:T(8,128)(2,1)S(1)} %join.1.refs_0_), channel_id=1, source_target_pairs={{0,32},{16,48},{32,0},{48,16},{64,96},{80,112},{96,64},{112,80},{1... | collective-permute-start | bytes 688136 | tf_op jit(solution)/shard_map/ppermute | solution.py:347
  56.7 10.7 %collective-permute-start = (bf16[2,128,256]{2,1,0:T(8,128)(2,1)S(1)}, bf16[2,128,256]{2,1,0:T(8,128)(2,1)S(1)}, u32[]{:S(2)}, u32[]{:S(2)}) collective-permute-start(bf16[2,128,256]{2,1,0:T(8,128)(2,1)S(1)} %get-tuple-element.10.refs_4_.near), channel_id=1, source_target_pairs={{0,256},{16,272},{32,288},{48,304},{64,320},{80,336},{96,352},{112... | collective-permute-start | bytes 393224 | tf_op jit(solution)/shard_map/ppermute | solution.py:338
  67.4 18.1 %copy-start.1 = (bf16[4,2,8,1792]{3,2,1,0:T(8,128)(2,1)}, bf16[4,2,8,1792]{3,2,1,0:T(8,128)(2,1)S(1)}, u32[]{:S(2)}) copy-start(bf16[4,2,8,1792]{3,2,1,0:T(8,128)(2,1)S(1)} %collective-permute-done.6.refs_2_.refs_3_) | copy-start | bytes 688132
  67.5 18.0 %copy-start.2 = (bf16[4,2,8,1792]{3,2,1,0:T(8,128)(2,1)}, bf16[4,2,8,1792]{3,2,1,0:T(8,128)(2,1)S(1)}, u32[]{:S(2)}) copy-start(bf16[4,2,8,1792]{3,2,1,0:T(8,128)(2,1)S(1)} %collective-permute-done.5.refs_1_.refs_2_) | copy-start | bytes 688132
  67.5 18.0 %copy-start.3 = (bf16[4,2,8,1792]{3,2,1,0:T(8,128)(2,1)}, bf16[4,2,8,1792]{3,2,1,0:T(8,128)(2,1)S(1)}, u32[]{:S(2)}) copy-start(bf16[4,2,8,1792]{3,2,1,0:T(8,128)(2,1)S(1)} %collective-permute-done.4.refs_0_.refs_1_) | copy-start | bytes 688132
  68.9 16.6 %all-to-all-start.2 = ((bf16[64,8,384]{2,1,0:T(8,128)(2,1)}), bf16[64,8,384]{2,1,0:T(8,128)(2,1)}, u32[]{:S(2)}, u32[]{:S(2)}) async-start(bf16[64,8,384]{2,1,0:T(8,128)(2,1)} %moment.1), calls=%async_computation.2 | async-start | bytes 786432 | tf_op jit(solution)/shard_map/all_to_all | solution.py:356
  74.5 8.8 %collective-permute-start.7 = (bf16[4,2,8,1792]{3,2,1,0:T(8,128)(2,1)S(1)}, bf16[4,2,8,1792]{3,2,1,0:T(8,128)(2,1)S(1)}, u32[]{:S(2)}, u32[]{:S(2)}) collective-permute-start(bf16[4,2,8,1792]{3,2,1,0:T(8,128)(2,1)S(1)} %join.1.refs_0_), channel_id=1, source_target_pairs={{0,16},{16,0},{32,48},{48,32},{64,80},{80,64},{96,112},{112,96},{1... | collective-permute-start | bytes 688136 | tf_op jit(solution)/shard_map/ppermute | solution.py:357
  77.1 6.3 %collective-permute-start.10 = (bf16[4,2,8,1792]{3,2,1,0:T(8,128)(2,1)S(1)}, bf16[4,2,8,1792]{3,2,1,0:T(8,128)(2,1)S(1)}, u32[]{:S(2)}, u32[]{:S(2)}) collective-permute-start(bf16[4,2,8,1792]{3,2,1,0:T(8,128)(2,1)S(1)} %collective-permute-done.6.refs_2_.refs_3_), channel_id=1, source_target_pairs={{0,16},{16,0},{32,48},{48,32},{64,80},{80,64},{96,112},{112,96},{1... | collective-permute-start | bytes 688136 | tf_op jit(solution)/shard_map/ppermute | solution.py:357
  79.0 4.4 %collective-permute-start.9 = (bf16[4,2,8,1792]{3,2,1,0:T(8,128)(2,1)S(1)}, bf16[4,2,8,1792]{3,2,1,0:T(8,128)(2,1)S(1)}, u32[]{:S(2)}, u32[]{:S(2)}) collective-permute-start(bf16[4,2,8,1792]{3,2,1,0:T(8,128)(2,1)S(1)} %collective-permute-done.5.refs_1_.refs_2_), channel_id=1, source_target_pairs={{0,16},{16,0},{32,48},{48,32},{64,80},{80,64},{96,112},{112,96},{1... | collective-permute-start | bytes 688136 | tf_op jit(solution)/shard_map/ppermute | solution.py:357
  81.4 3.5 %collective-permute-start.8 = (bf16[4,2,8,1792]{3,2,1,0:T(8,128)(2,1)S(1)}, bf16[4,2,8,1792]{3,2,1,0:T(8,128)(2,1)}, u32[]{:S(2)}, u32[]{:S(2)}) collective-permute-start(bf16[4,2,8,1792]{3,2,1,0:T(8,128)(2,1)S(1)} %collective-permute-done.4.refs_0_.refs_1_), channel_id=1, source_target_pairs={{0,16},{16,0},{32,48},{48,32},{64,80},{80,64},{96,112},{112,96},{1... | collective-permute-start | bytes 688136 | tf_op jit(solution)/shard_map/ppermute | solution.py:357
  83.4 2.1 %copy-start.5 = (bf16[4,2,8,1792]{3,2,1,0:T(8,128)(2,1)}, bf16[4,2,8,1792]{3,2,1,0:T(8,128)(2,1)S(1)}, u32[]{:S(2)}) copy-start(bf16[4,2,8,1792]{3,2,1,0:T(8,128)(2,1)S(1)} %collective-permute-done.7.refs_4_) | copy-start | bytes 688132
  83.4 0.7 copy-start.6
  84.1 0.7 copy-start.7

commit v4 on v3

--- a/solution.py
+++ b/solution.py
@@ -338,7 +338,7 @@
     far = lax.ppermute(near, "dp", swap(2, 0, 0))
     column = pl.pallas_call(
         join_kernel,
-        in_specs=[vmem] * 4 + [anywhere],
+        in_specs=[vmem] * 5,
         out_specs=vmem,
         out_shape=jax.ShapeDtypeStruct((4, *weights.shape), BF16),
         compiler_params=small,
@@ -347,7 +347,7 @@
     own = [column] + [lax.ppermute(column, "dp", swap(0, bits, 0)) for bits in (1, 2, 3)]
     send = pl.pallas_call(
         moment_kernel,
-        in_specs=[vmem, vmem, vmem] + [anywhere] * 3,
+        in_specs=[vmem] * 6,
         out_specs=vmem,
         out_shape=jax.ShapeDtypeStruct((64, 8, 384), BF16),
         compiler_params=small,
@@ -374,7 +374,7 @@
             jax.ShapeDtypeStruct((layers, block, rank), F32),
         ],
         scratch_shapes=[pltpu.VMEM((rank, cols), F32)],
-        compiler_params=roomy,
+        compiler_params=pltpu.CompilerParams(vmem_limit_bytes=51 * 2**20),
         name="update",
     )(received, proj, *own, *other)
 

time: 90 us -> 88.9 us (0.988)
  waiting for transfers between devices: 11 us -> 12.5 us
  local copies, waits for them, and re-layouts: 1.42 us -> 0.01 us
    unnamed x16 -> x2, local copies, waits for them, and re-layouts: 1.42 us -> 0.01 us
    ppermute x4, waiting for transfers between devices: 0.15 us -> 1.43 us  [shards(): other = [lax.ppermute(piece, 'dp', swap(0, 0, 1)) for piece in own]]
where the time goes in v4:
time: 88.9 us; the launch traced here: 88.2 us
  starting transfers between devices  60.8 us (68%)
  Pallas kernels  14.1 us (16%)
  waiting for transfers between devices  12.5 us (14%)
    all_to_all x2, starting transfers between devices, shards(): lax.all_to_all(send, BOTH, 0, 0, axis_index_groups=SLABS, tiled=True)  16 us
    all_to_all x1, starting transfers between devices, shards(): lax.all_to_all(send, BOTH, 0, 0, axis_index_groups=LINES, tiled=True)  13.2 us
    ppermute x3, starting transfers between devices, shards(): lax.ppermute(weights, 'dp', swap(bits, 0, 0))  9.6 us
    ppermute x3, starting transfers between devices, shards(): lax.ppermute(column, 'dp', swap(0, bits, 0))  8.98 us
    ppermute x4, starting transfers between devices, shards(): other = [lax.ppermute(piece, 'dp', swap(0, 0, 1)) for piece in own]  8.72 us
    pallas_call x1, Pallas kernels, shards(): pl.pallas_call(functools.partial(project_kernel, spread=spread), in_specs...  8.49 us
    ppermute x1, waiting for transfers between devices, shards(): far = lax.ppermute(near, 'dp', swap(2, 0, 0))  6.42 us
    all_to_all x2, waiting for transfers between devices, shards(): lax.all_to_all(send, BOTH, 0, 0, axis_index_groups=SLABS, tiled=True)  4.67 us
  transfers between devices with their start and end apart: 14, of which 4 were waited for; matrix products, arithmetic and copies ran while one was open for 0% of the time, Pallas kernels for 1%

profile of v4, /device:TPU:1, one launch (start us, length us, event | category | flops | bytes accessed | tf_op | source)
XLA Modules:
  0.0 88.2 jit_solution(6899138618097673108)
XLA Ops:
  0.6 8.5 %project.1 = (bf16[2,256,1792]{2,1,0:T(8,128)(2,1)}, bf16[64,8,640]{2,1,0:T(8,128)(2,1)}, bf16[2,8,1792]{2,1,0:T(8,128)(2,1)}) custom-call(s32[2]{0:T(128)} %seeds.1, s32[2]{0:T(128)} %old_seeds.1, bf16[1,2,256,1792]{3,2,1,0:T(8,128)(2,1)} %grads_hbm.1, f32[2,8,256]{2,1,0:T(8,128)} %first_hbm.1, f32[2,8,256]{2,1,0:T(8,128)} %second_hbm.1, ...), custom_call_target="tpu_custom_call" | custom-call | flops 8000000000 | bytes 6000000 | tf_op jit(solution)/shard_map/project/pallas_call | solution.py:295
  9.1 11.1 %all-to-all-start = ((bf16[64,8,640]{2,1,0:T(8,128)(2,1)}), bf16[64,8,640]{2,1,0:T(8,128)(2,1)S(1)}, u32[]{:S(2)}, u32[]{:S(2)}) async-start(bf16[64,8,640]{2,1,0:T(8,128)(2,1)} %get-tuple-element.8), calls=%async_computation | async-start | bytes 1310720 | tf_op jit(solution)/shard_map/all_to_all | solution.py:324
  20.2 5.5 %collective-permute-start.3 = (bf16[2,8,1792]{2,1,0:T(8,128)(2,1)}, bf16[2,8,1792]{2,1,0:T(8,128)(2,1)S(1)}, u32[]{:S(2)}, u32[]{:S(2)}) collective-permute-start(bf16[2,8,1792]{2,1,0:T(8,128)(2,1)} %get-tuple-element.11.refs_0_), channel_id=1, source_target_pairs={{0,384},{16,400},{32,416},{48,432},{64,448},{80,464},{96,480},{112... | collective-permute-start | bytes 172040 | tf_op jit(solution)/shard_map/ppermute | solution.py:325
  25.7 1.9 %collective-permute-start.2 = (bf16[2,8,1792]{2,1,0:T(8,128)(2,1)}, bf16[2,8,1792]{2,1,0:T(8,128)(2,1)S(1)}, u32[]{:S(2)}, u32[]{:S(2)}) collective-permute-start(bf16[2,8,1792]{2,1,0:T(8,128)(2,1)} %get-tuple-element.11.refs_0_), channel_id=1, source_target_pairs={{0,256},{16,272},{32,288},{48,304},{64,320},{80,336},{96,352},{112... | collective-permute-start | bytes 172040 | tf_op jit(solution)/shard_map/ppermute | solution.py:325
  27.7 2.2 %collective-permute-start.1 = (bf16[2,8,1792]{2,1,0:T(8,128)(2,1)}, bf16[2,8,1792]{2,1,0:T(8,128)(2,1)S(1)}, u32[]{:S(2)}, u32[]{:S(2)}) collective-permute-start(bf16[2,8,1792]{2,1,0:T(8,128)(2,1)} %get-tuple-element.11.refs_0_), channel_id=1, source_target_pairs={{0,128},{16,144},{32,160},{48,176},{64,192},{80,208},{96,224},{112... | collective-permute-start | bytes 172040 | tf_op jit(solution)/shard_map/ppermute | solution.py:325
  29.9 3.9 %all-to-all-done.received = bf16[64,8,640]{2,1,0:T(8,128)(2,1)S(1)} async-done(((bf16[64,8,640]{2,1,0:T(8,128)(2,1)}), bf16[64,8,640]{2,1,0:T(8,128)(2,1)S(1)}, u32[]{:S(2)}, u32[]{:S(2)}) %all-to-all-start) | async-done | bytes 655392 | tf_op jit(solution)/shard_map/all_to_all | solution.py:324
  33.7 0.7 slab_sum.1
  34.5 13.2 %all-to-all-start.1 = ((bf16[8,8,512]{2,1,0:T(8,128)(2,1)}), bf16[8,8,512]{2,1,0:T(8,128)(2,1)S(1)}, u32[]{:S(2)}, u32[]{:S(2)}) async-start(bf16[8,8,512]{2,1,0:T(8,128)(2,1)} %get-tuple-element.9), calls=%async_computation.1 | async-start | bytes 131072 | tf_op jit(solution)/shard_map/all_to_all | solution.py:337
  47.7 0.0 collective-permute-done.3.refs_3_
  47.7 0.0 collective-permute-done.2.refs_2_
  47.7 2.7 %collective-permute-start.6 = (bf16[4,2,8,1792]{3,2,1,0:T(8,128)(2,1)S(1)}, bf16[4,2,8,1792]{3,2,1,0:T(8,128)(2,1)S(1)}, u32[]{:S(2)}, u32[]{:S(2)}) collective-permute-start(bf16[4,2,8,1792]{3,2,1,0:T(8,128)(2,1)S(1)} %join.1.refs_0_), channel_id=1, source_target_pairs={{0,96},{16,112},{32,64},{48,80},{64,32},{80,48},{96,0},{112,16},{1... | collective-permute-start | bytes 688136 | tf_op jit(solution)/shard_map/ppermute | solution.py:347
  50.4 3.1 %collective-permute-start.5 = (bf16[4,2,8,1792]{3,2,1,0:T(8,128)(2,1)S(1)}, bf16[4,2,8,1792]{3,2,1,0:T(8,128)(2,1)S(1)}, u32[]{:S(2)}, u32[]{:S(2)}) collective-permute-start(bf16[4,2,8,1792]{3,2,1,0:T(8,128)(2,1)S(1)} %join.1.refs_0_), channel_id=1, source_target_pairs={{0,64},{16,80},{32,96},{48,112},{64,0},{80,16},{96,32},{112,48},{1... | collective-permute-start | bytes 688136 | tf_op jit(solution)/shard_map/ppermute | solution.py:347
  53.6 3.2 %collective-permute-start.4 = (bf16[4,2,8,1792]{3,2,1,0:T(8,128)(2,1)S(1)}, bf16[4,2,8,1792]{3,2,1,0:T(8,128)(2,1)S(1)}, u32[]{:S(2)}, u32[]{:S(2)}) collective-permute-start(bf16[4,2,8,1792]{3,2,1,0:T(8,128)(2,1)S(1)} %join.1.refs_0_), channel_id=1, source_target_pairs={{0,32},{16,48},{32,0},{48,16},{64,96},{80,112},{96,64},{112,80},{1... | collective-permute-start | bytes 688136 | tf_op jit(solution)/shard_map/ppermute | solution.py:347
  56.7 4.3 %collective-permute-start = (bf16[2,128,256]{2,1,0:T(8,128)(2,1)S(1)}, bf16[2,128,256]{2,1,0:T(8,128)(2,1)S(1)}, u32[]{:S(2)}, u32[]{:S(2)}) collective-permute-start(bf16[2,128,256]{2,1,0:T(8,128)(2,1)S(1)} %get-tuple-element.10.refs_4_.near), channel_id=1, source_target_pairs={{0,256},{16,272},{32,288},{48,304},{64,320},{80,336},{96,352},{112... | collective-permute-start | bytes 393224 | tf_op jit(solution)/shard_map/ppermute | solution.py:338
  61.0 6.4 %collective-permute-done.far = bf16[2,128,256]{2,1,0:T(8,128)(2,1)S(1)} collective-permute-done((bf16[2,128,256]{2,1,0:T(8,128)(2,1)S(1)}, bf16[2,128,256]{2,1,0:T(8,128)(2,1)S(1)}, u32[]{:S(2)}, u32[]{:S(2)}) %collective-permute-start) | collective-permute-done | bytes 131104 | tf_op jit(solution)/shard_map/ppermute | solution.py:338
  67.5 1.4 %moment.1 = bf16[64,8,384]{2,1,0:T(8,128)(2,1)} custom-call(bf16[8,8,512]{2,1,0:T(8,128)(2,1)S(1)} %all-to-all-done.1.received, bf16[2,128,256]{2,1,0:T(8,128)(2,1)S(1)} %get-tuple-element.10.refs_4_.near, bf16[2,128,256]{2,1,0:T(8,128)(2,1)S(1)} %collective-permute-done.far, bf16[4,2,8,1792]{3,2,1,0:T(8,128)(2,1)S(1)} %collective-permute-done.4.refs_0_.refs_1_, ...), custom_call_target="tpu_custom_call" | custom-call | tf_op jit(solution)/shard_map/moment/pallas_call | solution.py:348
  68.8 4.9 %all-to-all-start.2 = ((bf16[64,8,384]{2,1,0:T(8,128)(2,1)}), bf16[64,8,384]{2,1,0:T(8,128)(2,1)S(1)}, u32[]{:S(2)}, u32[]{:S(2)}) async-start(bf16[64,8,384]{2,1,0:T(8,128)(2,1)} %moment.1), calls=%async_computation.2 | async-start | bytes 786432 | tf_op jit(solution)/shard_map/all_to_all | solution.py:356
  73.7 2.5 %collective-permute-start.7 = (bf16[4,2,8,1792]{3,2,1,0:T(8,128)(2,1)S(1)}, bf16[4,2,8,1792]{3,2,1,0:T(8,128)(2,1)S(1)}, u32[]{:S(2)}, u32[]{:S(2)}) collective-permute-start(bf16[4,2,8,1792]{3,2,1,0:T(8,128)(2,1)S(1)} %join.1.refs_0_), channel_id=1, source_target_pairs={{0,16},{16,0},{32,48},{48,32},{64,80},{80,64},{96,112},{112,96},{1... | collective-permute-start | bytes 688136 | tf_op jit(solution)/shard_map/ppermute | solution.py:357
  76.2 1.9 %collective-permute-start.10 = (bf16[4,2,8,1792]{3,2,1,0:T(8,128)(2,1)S(1)}, bf16[4,2,8,1792]{3,2,1,0:T(8,128)(2,1)S(1)}, u32[]{:S(2)}, u32[]{:S(2)}) collective-permute-start(bf16[4,2,8,1792]{3,2,1,0:T(8,128)(2,1)S(1)} %collective-permute-done.6.refs_2_.refs_3_), channel_id=1, source_target_pairs={{0,16},{16,0},{32,48},{48,32},{64,80},{80,64},{96,112},{112,96},{1... | collective-permute-start | bytes 688136 | tf_op jit(solution)/shard_map/ppermute | solution.py:357
  78.1 2.4 %collective-permute-start.9 = (bf16[4,2,8,1792]{3,2,1,0:T(8,128)(2,1)S(1)}, bf16[4,2,8,1792]{3,2,1,0:T(8,128)(2,1)S(1)}, u32[]{:S(2)}, u32[]{:S(2)}) collective-permute-start(bf16[4,2,8,1792]{3,2,1,0:T(8,128)(2,1)S(1)} %collective-permute-done.5.refs_1_.refs_2_), channel_id=1, source_target_pairs={{0,16},{16,0},{32,48},{48,32},{64,80},{80,64},{96,112},{112,96},{1... | collective-permute-start | bytes 688136 | tf_op jit(solution)/shard_map/ppermute | solution.py:357
  80.6 1.9 %collective-permute-start.8 = (bf16[4,2,8,1792]{3,2,1,0:T(8,128)(2,1)S(1)}, bf16[4,2,8,1792]{3,2,1,0:T(8,128)(2,1)S(1)}, u32[]{:S(2)}, u32[]{:S(2)}) collective-permute-start(bf16[4,2,8,1792]{3,2,1,0:T(8,128)(2,1)S(1)} %collective-permute-done.4.refs_0_.refs_1_), channel_id=1, source_target_pairs={{0,16},{16,0},{32,48},{48,32},{64,80},{80,64},{96,112},{112,96},{1... | collective-permute-start | bytes 688136 | tf_op jit(solution)/shard_map/ppermute | solution.py:357
  82.5 1.4 %collective-permute-done.8.refs_5_ = bf16[4,2,8,1792]{3,2,1,0:T(8,128)(2,1)S(1)} collective-permute-done((bf16[4,2,8,1792]{3,2,1,0:T(8,128)(2,1)S(1)}, bf16[4,2,8,1792]{3,2,1,0:T(8,128)(2,1)S(1)}, u32[]{:S(2)}, u32[]{:S(2)}) %collective-permute-start.8) | collective-permute-done | bytes 229408 | tf_op jit(solution)/shard_map/ppermute | solution.py:357
  83.9 0.8 all-to-all-done.2.received
  84.8 3.5 %update.1 = (bf16[2,256,1792]{2,1,0:T(8,128)(2,1)}, f32[2,8,256]{2,1,0:T(8,128)}, f32[2,8,256]{2,1,0:T(8,128)}) custom-call(bf16[64,8,384]{2,1,0:T(8,128)(2,1)S(1)} %all-to-all-done.2.received, bf16[2,256,1792]{2,1,0:T(8,128)(2,1)} %get-tuple-element.12.proj, bf16[4,2,8,1792]{3,2,1,0:T(8,128)(2,1)S(1)} %join.1.refs_0_, ...), custom_call_target="tpu_custom_call" | custom-call | tf_op jit(solution)/shard_map/update/pallas_call | solution.py:362
  (11 shorter events, 0.0 us)
Async XLA Ops:
  9.1 38.6 %copy-start = (bf16[2,8,1792]{2,1,0:T(8,128)(2,1)S(1)}, bf16[2,8,1792]{2,1,0:T(8,128)(2,1)}, u32[]{:S(2)}) copy-start(bf16[2,8,1792]{2,1,0:T(8,128)(2,1)} %get-tuple-element.11.refs_0_) | copy-start | bytes 172036
  9.1 24.6 %all-to-all-start = ((bf16[64,8,640]{2,1,0:T(8,128)(2,1)}), bf16[64,8,640]{2,1,0:T(8,128)(2,1)S(1)}, u32[]{:S(2)}, u32[]{:S(2)}) async-start(bf16[64,8,640]{2,1,0:T(8,128)(2,1)} %get-tuple-element.8), calls=%async_computation | async-start | bytes 1310720 | tf_op jit(solution)/shard_map/all_to_all | solution.py:324
  20.2 27.4 %collective-permute-start.3 = (bf16[2,8,1792]{2,1,0:T(8,128)(2,1)}, bf16[2,8,1792]{2,1,0:T(8,128)(2,1)S(1)}, u32[]{:S(2)}, u32[]{:S(2)}) collective-permute-start(bf16[2,8,1792]{2,1,0:T(8,128)(2,1)} %get-tuple-element.11.refs_0_), channel_id=1, source_target_pairs={{0,384},{16,400},{32,416},{48,432},{64,448},{80,464},{96,480},{112... | collective-permute-start | bytes 172040 | tf_op jit(solution)/shard_map/ppermute | solution.py:325
  25.7 21.9 %collective-permute-start.2 = (bf16[2,8,1792]{2,1,0:T(8,128)(2,1)}, bf16[2,8,1792]{2,1,0:T(8,128)(2,1)S(1)}, u32[]{:S(2)}, u32[]{:S(2)}) collective-permute-start(bf16[2,8,1792]{2,1,0:T(8,128)(2,1)} %get-tuple-element.11.refs_0_), channel_id=1, source_target_pairs={{0,256},{16,272},{32,288},{48,304},{64,320},{80,336},{96,352},{112... | collective-permute-start | bytes 172040 | tf_op jit(solution)/shard_map/ppermute | solution.py:325
  27.7 20.0 %collective-permute-start.1 = (bf16[2,8,1792]{2,1,0:T(8,128)(2,1)}, bf16[2,8,1792]{2,1,0:T(8,128)(2,1)S(1)}, u32[]{:S(2)}, u32[]{:S(2)}) collective-permute-start(bf16[2,8,1792]{2,1,0:T(8,128)(2,1)} %get-tuple-element.11.refs_0_), channel_id=1, source_target_pairs={{0,128},{16,144},{32,160},{48,176},{64,192},{80,208},{96,224},{112... | collective-permute-start | bytes 172040 | tf_op jit(solution)/shard_map/ppermute | solution.py:325
  34.5 33.0 %all-to-all-start.1 = ((bf16[8,8,512]{2,1,0:T(8,128)(2,1)}), bf16[8,8,512]{2,1,0:T(8,128)(2,1)S(1)}, u32[]{:S(2)}, u32[]{:S(2)}) async-start(bf16[8,8,512]{2,1,0:T(8,128)(2,1)} %get-tuple-element.9), calls=%async_computation.1 | async-start | bytes 131072 | tf_op jit(solution)/shard_map/all_to_all | solution.py:337
  47.7 19.7 %collective-permute-start.6 = (bf16[4,2,8,1792]{3,2,1,0:T(8,128)(2,1)S(1)}, bf16[4,2,8,1792]{3,2,1,0:T(8,128)(2,1)S(1)}, u32[]{:S(2)}, u32[]{:S(2)}) collective-permute-start(bf16[4,2,8,1792]{3,2,1,0:T(8,128)(2,1)S(1)} %join.1.refs_0_), channel_id=1, source_target_pairs={{0,96},{16,112},{32,64},{48,80},{64,32},{80,48},{96,0},{112,16},{1... | collective-permute-start | bytes 688136 | tf_op jit(solution)/shard_map/ppermute | solution.py:347
  50.4 17.0 %collective-permute-start.5 = (bf16[4,2,8,1792]{3,2,1,0:T(8,128)(2,1)S(1)}, bf16[4,2,8,1792]{3,2,1,0:T(8,128)(2,1)S(1)}, u32[]{:S(2)}, u32[]{:S(2)}) collective-permute-start(bf16[4,2,8,1792]{3,2,1,0:T(8,128)(2,1)S(1)} %join.1.refs_0_), channel_id=1, source_target_pairs={{0,64},{16,80},{32,96},{48,112},{64,0},{80,16},{96,32},{112,48},{1... | collective-permute-start | bytes 688136 | tf_op jit(solution)/shard_map/ppermute | solution.py:347
  53.6 13.9 %collective-permute-start.4 = (bf16[4,2,8,1792]{3,2,1,0:T(8,128)(2,1)S(1)}, bf16[4,2,8,1792]{3,2,1,0:T(8,128)(2,1)S(1)}, u32[]{:S(2)}, u32[]{:S(2)}) collective-permute-start(bf16[4,2,8,1792]{3,2,1,0:T(8,128)(2,1)S(1)} %join.1.refs_0_), channel_id=1, source_target_pairs={{0,32},{16,48},{32,0},{48,16},{64,96},{80,112},{96,64},{112,80},{1... | collective-permute-start | bytes 688136 | tf_op jit(solution)/shard_map/ppermute | solution.py:347
  56.7 10.7 %collective-permute-start = (bf16[2,128,256]{2,1,0:T(8,128)(2,1)S(1)}, bf16[2,128,256]{2,1,0:T(8,128)(2,1)S(1)}, u32[]{:S(2)}, u32[]{:S(2)}) collective-permute-start(bf16[2,128,256]{2,1,0:T(8,128)(2,1)S(1)} %get-tuple-element.10.refs_4_.near), channel_id=1, source_target_pairs={{0,256},{16,272},{32,288},{48,304},{64,320},{80,336},{96,352},{112... | collective-permute-start | bytes 393224 | tf_op jit(solution)/shard_map/ppermute | solution.py:338
  68.8 15.9 %all-to-all-start.2 = ((bf16[64,8,384]{2,1,0:T(8,128)(2,1)}), bf16[64,8,384]{2,1,0:T(8,128)(2,1)S(1)}, u32[]{:S(2)}, u32[]{:S(2)}) async-start(bf16[64,8,384]{2,1,0:T(8,128)(2,1)} %moment.1), calls=%async_computation.2 | async-start | bytes 786432 | tf_op jit(solution)/shard_map/all_to_all | solution.py:356
  73.7 8.8 %collective-permute-start.7 = (bf16[4,2,8,1792]{3,2,1,0:T(8,128)(2,1)S(1)}, bf16[4,2,8,1792]{3,2,1,0:T(8,128)(2,1)S(1)}, u32[]{:S(2)}, u32[]{:S(2)}) collective-permute-start(bf16[4,2,8,1792]{3,2,1,0:T(8,128)(2,1)S(1)} %join.1.refs_0_), channel_id=1, source_target_pairs={{0,16},{16,0},{32,48},{48,32},{64,80},{80,64},{96,112},{112,96},{1... | collective-permute-start | bytes 688136 | tf_op jit(solution)/shard_map/ppermute | solution.py:357
  76.2 6.3 %collective-permute-start.10 = (bf16[4,2,8,1792]{3,2,1,0:T(8,128)(2,1)S(1)}, bf16[4,2,8,1792]{3,2,1,0:T(8,128)(2,1)S(1)}, u32[]{:S(2)}, u32[]{:S(2)}) collective-permute-start(bf16[4,2,8,1792]{3,2,1,0:T(8,128)(2,1)S(1)} %collective-permute-done.6.refs_2_.refs_3_), channel_id=1, source_target_pairs={{0,16},{16,0},{32,48},{48,32},{64,80},{80,64},{96,112},{112,96},{1... | collective-permute-start | bytes 688136 | tf_op jit(solution)/shard_map/ppermute | solution.py:357
  78.1 4.4 %collective-permute-start.9 = (bf16[4,2,8,1792]{3,2,1,0:T(8,128)(2,1)S(1)}, bf16[4,2,8,1792]{3,2,1,0:T(8,128)(2,1)S(1)}, u32[]{:S(2)}, u32[]{:S(2)}) collective-permute-start(bf16[4,2,8,1792]{3,2,1,0:T(8,128)(2,1)S(1)} %collective-permute-done.5.refs_1_.refs_2_), channel_id=1, source_target_pairs={{0,16},{16,0},{32,48},{48,32},{64,80},{80,64},{96,112},{112,96},{1... | collective-permute-start | bytes 688136 | tf_op jit(solution)/shard_map/ppermute | solution.py:357
  80.6 3.4 %collective-permute-start.8 = (bf16[4,2,8,1792]{3,2,1,0:T(8,128)(2,1)S(1)}, bf16[4,2,8,1792]{3,2,1,0:T(8,128)(2,1)S(1)}, u32[]{:S(2)}, u32[]{:S(2)}) collective-permute-start(bf16[4,2,8,1792]{3,2,1,0:T(8,128)(2,1)S(1)} %collective-permute-done.4.refs_0_.refs_1_), channel_id=1, source_target_pairs={{0,16},{16,0},{32,48},{48,32},{64,80},{80,64},{96,112},{112,96},{1... | collective-permute-start | bytes 688136 | tf_op jit(solution)/shard_map/ppermute | solution.py:357

commit v5 on v4

--- a/solution.py
+++ b/solution.py
@@ -289,7 +289,7 @@
     vmem = pl.BlockSpec(memory_space=pltpu.VMEM)
     hbm = pl.BlockSpec(memory_space=pltpu.HBM)
     anywhere = pl.BlockSpec(memory_space=pl.ANY)
-    roomy = pltpu.CompilerParams(vmem_limit_bytes=251 * 2**18)
+    roomy = pltpu.CompilerParams(vmem_limit_bytes=50 * 2**20)
     small = pltpu.CompilerParams(vmem_limit_bytes=8 * 2**20)
 
     proj, send, weights = pl.pallas_call(

time: 88.9 us -> 94.2 us (1.060)
  local copies, waits for them, and re-layouts: 0.01 us -> 4.81 us
    unnamed x2 -> x12, local copies, waits for them, and re-layouts: 0.01 us -> 4.81 us
where the time goes in v5:
time: 94.2 us; the launch traced here: 93.3 us
  starting transfers between devices  60.6 us (64%)
  Pallas kernels  14.5 us (15%)
  waiting for transfers between devices  12.5 us (13%)
  local copies, waits for them, and re-layouts  4.81 us (5%)
    all_to_all x2, starting transfers between devices, shards(): lax.all_to_all(send, BOTH, 0, 0, axis_index_groups=SLABS, tiled=True)  15.8 us
    all_to_all x1, starting transfers between devices, shards(): lax.all_to_all(send, BOTH, 0, 0, axis_index_groups=LINES, tiled=True)  13.2 us
    ppermute x3, starting transfers between devices, shards(): lax.ppermute(weights, 'dp', swap(bits, 0, 0))  9.61 us
    ppermute x3, starting transfers between devices, shards(): lax.ppermute(column, 'dp', swap(0, bits, 0))  8.98 us
    pallas_call x1, Pallas kernels, shards(): pl.pallas_call(functools.partial(project_kernel, spread=spread), in_specs...  8.93 us
    ppermute x4, starting transfers between devices, shards(): other = [lax.ppermute(piece, 'dp', swap(0, 0, 1)) for piece in own]  8.72 us
    ppermute x1, waiting for transfers between devices, shards(): far = lax.ppermute(near, 'dp', swap(2, 0, 0))  6.42 us
    unnamed x12, local copies, waits for them, and re-layouts  4.81 us
  transfers between devices with their start and end apart: 14, of which 4 were waited for; matrix products, arithmetic and copies ran while one was open for 0% of the time, Pallas kernels for 1%

profile of v5, /device:TPU:1, one launch (start us, length us, event | category | flops | bytes accessed | tf_op | source)
XLA Modules:
  0.0 93.3 jit_solution(2966707086836520295)
XLA Ops:
  0.6 0.8 copy-done.1
  4.2 8.9 %project.1 = (bf16[2,256,1792]{2,1,0:T(8,128)(2,1)S(1)}, bf16[64,8,640]{2,1,0:T(8,128)(2,1)}, bf16[2,8,1792]{2,1,0:T(8,128)(2,1)S(1)}) custom-call(s32[2]{0:T(128)S(1)} %copy-done.4, s32[2]{0:T(128)S(1)} %copy-done.5, bf16[1,2,256,1792]{3,2,1,0:T(8,128)(2,1)} %grads_hbm.1, f32[2,8,256]{2,1,0:T(8,128)S(1)} %copy-done.2, f32[2,8,256]{2,1,0:T(8,128)S(1)} %copy-done.3, ...), custom_call_target="tpu_custom_call" | custom-call | flops 8000000000 | bytes 6000000 | tf_op jit(solution)/shard_map/project/pallas_call | solution.py:295
  13.1 1.3 %copy-done = bf16[2,256,1792]{2,1,0:T(8,128)(2,1)} copy-done((bf16[2,256,1792]{2,1,0:T(8,128)(2,1)}, bf16[2,256,1792]{2,1,0:T(8,128)(2,1)S(1)}, u32[]{:S(2)}) %copy-start) | copy-done | bytes 1835032
  14.4 10.9 %all-to-all-start = ((bf16[64,8,640]{2,1,0:T(8,128)(2,1)}), bf16[64,8,640]{2,1,0:T(8,128)(2,1)S(1)}, u32[]{:S(2)}, u32[]{:S(2)}) async-start(bf16[64,8,640]{2,1,0:T(8,128)(2,1)} %get-tuple-element.8), calls=%async_computation | async-start | bytes 1310720 | tf_op jit(solution)/shard_map/all_to_all | solution.py:324
  25.4 5.5 %collective-permute-start.3 = (bf16[2,8,1792]{2,1,0:T(8,128)(2,1)S(1)}, bf16[2,8,1792]{2,1,0:T(8,128)(2,1)S(1)}, u32[]{:S(2)}, u32[]{:S(2)}) collective-permute-start(bf16[2,8,1792]{2,1,0:T(8,128)(2,1)S(1)} %get-tuple-element.11.refs_0_), channel_id=1, source_target_pairs={{0,384},{16,400},{32,416},{48,432},{64,448},{80,464},{96,480},{112... | collective-permute-start | bytes 172040 | tf_op jit(solution)/shard_map/ppermute | solution.py:325
  30.9 1.9 %collective-permute-start.2 = (bf16[2,8,1792]{2,1,0:T(8,128)(2,1)S(1)}, bf16[2,8,1792]{2,1,0:T(8,128)(2,1)S(1)}, u32[]{:S(2)}, u32[]{:S(2)}) collective-permute-start(bf16[2,8,1792]{2,1,0:T(8,128)(2,1)S(1)} %get-tuple-element.11.refs_0_), channel_id=1, source_target_pairs={{0,256},{16,272},{32,288},{48,304},{64,320},{80,336},{96,352},{112... | collective-permute-start | bytes 172040 | tf_op jit(solution)/shard_map/ppermute | solution.py:325
  32.8 2.2 %collective-permute-start.1 = (bf16[2,8,1792]{2,1,0:T(8,128)(2,1)S(1)}, bf16[2,8,1792]{2,1,0:T(8,128)(2,1)S(1)}, u32[]{:S(2)}, u32[]{:S(2)}) collective-permute-start(bf16[2,8,1792]{2,1,0:T(8,128)(2,1)S(1)} %get-tuple-element.11.refs_0_), channel_id=1, source_target_pairs={{0,128},{16,144},{32,160},{48,176},{64,192},{80,208},{96,224},{112... | collective-permute-start | bytes 172040 | tf_op jit(solution)/shard_map/ppermute | solution.py:325
  35.0 3.9 %all-to-all-done.received = bf16[64,8,640]{2,1,0:T(8,128)(2,1)S(1)} async-done(((bf16[64,8,640]{2,1,0:T(8,128)(2,1)}), bf16[64,8,640]{2,1,0:T(8,128)(2,1)S(1)}, u32[]{:S(2)}, u32[]{:S(2)}) %all-to-all-start) | async-done | bytes 655392 | tf_op jit(solution)/shard_map/all_to_all | solution.py:324
  38.9 0.7 slab_sum.1
  39.6 13.2 %all-to-all-start.1 = ((bf16[8,8,512]{2,1,0:T(8,128)(2,1)}), bf16[8,8,512]{2,1,0:T(8,128)(2,1)S(1)}, u32[]{:S(2)}, u32[]{:S(2)}) async-start(bf16[8,8,512]{2,1,0:T(8,128)(2,1)} %get-tuple-element.9), calls=%async_computation.1 | async-start | bytes 131072 | tf_op jit(solution)/shard_map/all_to_all | solution.py:337
  52.9 2.7 %collective-permute-start.6 = (bf16[4,2,8,1792]{3,2,1,0:T(8,128)(2,1)S(1)}, bf16[4,2,8,1792]{3,2,1,0:T(8,128)(2,1)S(1)}, u32[]{:S(2)}, u32[]{:S(2)}) collective-permute-start(bf16[4,2,8,1792]{3,2,1,0:T(8,128)(2,1)S(1)} %join.1.refs_0_), channel_id=1, source_target_pairs={{0,96},{16,112},{32,64},{48,80},{64,32},{80,48},{96,0},{112,16},{1... | collective-permute-start | bytes 688136 | tf_op jit(solution)/shard_map/ppermute | solution.py:347
  55.5 3.1 %collective-permute-start.5 = (bf16[4,2,8,1792]{3,2,1,0:T(8,128)(2,1)S(1)}, bf16[4,2,8,1792]{3,2,1,0:T(8,128)(2,1)S(1)}, u32[]{:S(2)}, u32[]{:S(2)}) collective-permute-start(bf16[4,2,8,1792]{3,2,1,0:T(8,128)(2,1)S(1)} %join.1.refs_0_), channel_id=1, source_target_pairs={{0,64},{16,80},{32,96},{48,112},{64,0},{80,16},{96,32},{112,48},{1... | collective-permute-start | bytes 688136 | tf_op jit(solution)/shard_map/ppermute | solution.py:347
  58.7 3.2 %collective-permute-start.4 = (bf16[4,2,8,1792]{3,2,1,0:T(8,128)(2,1)S(1)}, bf16[4,2,8,1792]{3,2,1,0:T(8,128)(2,1)S(1)}, u32[]{:S(2)}, u32[]{:S(2)}) collective-permute-start(bf16[4,2,8,1792]{3,2,1,0:T(8,128)(2,1)S(1)} %join.1.refs_0_), channel_id=1, source_target_pairs={{0,32},{16,48},{32,0},{48,16},{64,96},{80,112},{96,64},{112,80},{1... | collective-permute-start | bytes 688136 | tf_op jit(solution)/shard_map/ppermute | solution.py:347
  61.9 4.3 %collective-permute-start = (bf16[2,128,256]{2,1,0:T(8,128)(2,1)S(1)}, bf16[2,128,256]{2,1,0:T(8,128)(2,1)S(1)}, u32[]{:S(2)}, u32[]{:S(2)}) collective-permute-start(bf16[2,128,256]{2,1,0:T(8,128)(2,1)S(1)} %get-tuple-element.10.refs_4_.near), channel_id=1, source_target_pairs={{0,256},{16,272},{32,288},{48,304},{64,320},{80,336},{96,352},{112... | collective-permute-start | bytes 393224 | tf_op jit(solution)/shard_map/ppermute | solution.py:338
  66.1 6.4 %collective-permute-done.far = bf16[2,128,256]{2,1,0:T(8,128)(2,1)S(1)} collective-permute-done((bf16[2,128,256]{2,1,0:T(8,128)(2,1)S(1)}, bf16[2,128,256]{2,1,0:T(8,128)(2,1)S(1)}, u32[]{:S(2)}, u32[]{:S(2)}) %collective-permute-start) | collective-permute-done | bytes 131104 | tf_op jit(solution)/shard_map/ppermute | solution.py:338
  72.6 1.4 %moment.1 = bf16[64,8,384]{2,1,0:T(8,128)(2,1)} custom-call(bf16[8,8,512]{2,1,0:T(8,128)(2,1)S(1)} %all-to-all-done.1.received, bf16[2,128,256]{2,1,0:T(8,128)(2,1)S(1)} %get-tuple-element.10.refs_4_.near, bf16[2,128,256]{2,1,0:T(8,128)(2,1)S(1)} %collective-permute-done.far, bf16[4,2,8,1792]{3,2,1,0:T(8,128)(2,1)S(1)} %collective-permute-done.4.refs_0_.refs_1_, ...), custom_call_target="tpu_custom_call" | custom-call | tf_op jit(solution)/shard_map/moment/pallas_call | solution.py:348
  74.0 4.9 %all-to-all-start.2 = ((bf16[64,8,384]{2,1,0:T(8,128)(2,1)}), bf16[64,8,384]{2,1,0:T(8,128)(2,1)S(1)}, u32[]{:S(2)}, u32[]{:S(2)}) async-start(bf16[64,8,384]{2,1,0:T(8,128)(2,1)} %moment.1), calls=%async_computation.2 | async-start | bytes 786432 | tf_op jit(solution)/shard_map/all_to_all | solution.py:356
  78.8 2.5 %collective-permute-start.7 = (bf16[4,2,8,1792]{3,2,1,0:T(8,128)(2,1)S(1)}, bf16[4,2,8,1792]{3,2,1,0:T(8,128)(2,1)S(1)}, u32[]{:S(2)}, u32[]{:S(2)}) collective-permute-start(bf16[4,2,8,1792]{3,2,1,0:T(8,128)(2,1)S(1)} %join.1.refs_0_), channel_id=1, source_target_pairs={{0,16},{16,0},{32,48},{48,32},{64,80},{80,64},{96,112},{112,96},{1... | collective-permute-start | bytes 688136 | tf_op jit(solution)/shard_map/ppermute | solution.py:357
  81.3 1.9 %collective-permute-start.10 = (bf16[4,2,8,1792]{3,2,1,0:T(8,128)(2,1)S(1)}, bf16[4,2,8,1792]{3,2,1,0:T(8,128)(2,1)S(1)}, u32[]{:S(2)}, u32[]{:S(2)}) collective-permute-start(bf16[4,2,8,1792]{3,2,1,0:T(8,128)(2,1)S(1)} %collective-permute-done.6.refs_2_.refs_3_), channel_id=1, source_target_pairs={{0,16},{16,0},{32,48},{48,32},{64,80},{80,64},{96,112},{112,96},{1... | collective-permute-start | bytes 688136 | tf_op jit(solution)/shard_map/ppermute | solution.py:357
  83.3 2.4 %collective-permute-start.9 = (bf16[4,2,8,1792]{3,2,1,0:T(8,128)(2,1)S(1)}, bf16[4,2,8,1792]{3,2,1,0:T(8,128)(2,1)S(1)}, u32[]{:S(2)}, u32[]{:S(2)}) collective-permute-start(bf16[4,2,8,1792]{3,2,1,0:T(8,128)(2,1)S(1)} %collective-permute-done.5.refs_1_.refs_2_), channel_id=1, source_target_pairs={{0,16},{16,0},{32,48},{48,32},{64,80},{80,64},{96,112},{112,96},{1... | collective-permute-start | bytes 688136 | tf_op jit(solution)/shard_map/ppermute | solution.py:357
  85.7 1.9 %collective-permute-start.8 = (bf16[4,2,8,1792]{3,2,1,0:T(8,128)(2,1)S(1)}, bf16[4,2,8,1792]{3,2,1,0:T(8,128)(2,1)S(1)}, u32[]{:S(2)}, u32[]{:S(2)}) collective-permute-start(bf16[4,2,8,1792]{3,2,1,0:T(8,128)(2,1)S(1)} %collective-permute-done.4.refs_0_.refs_1_), channel_id=1, source_target_pairs={{0,16},{16,0},{32,48},{48,32},{64,80},{80,64},{96,112},{112,96},{1... | collective-permute-start | bytes 688136 | tf_op jit(solution)/shard_map/ppermute | solution.py:357
  87.6 1.4 %collective-permute-done.8.refs_5_ = bf16[4,2,8,1792]{3,2,1,0:T(8,128)(2,1)S(1)} collective-permute-done((bf16[4,2,8,1792]{3,2,1,0:T(8,128)(2,1)S(1)}, bf16[4,2,8,1792]{3,2,1,0:T(8,128)(2,1)S(1)}, u32[]{:S(2)}, u32[]{:S(2)}) %collective-permute-start.8) | collective-permute-done | bytes 229408 | tf_op jit(solution)/shard_map/ppermute | solution.py:357
  89.1 0.8 all-to-all-done.2.received
  89.9 3.5 %update.1 = (bf16[2,256,1792]{2,1,0:T(8,128)(2,1)}, f32[2,8,256]{2,1,0:T(8,128)}, f32[2,8,256]{2,1,0:T(8,128)}) custom-call(bf16[64,8,384]{2,1,0:T(8,128)(2,1)S(1)} %all-to-all-done.2.received, bf16[2,256,1792]{2,1,0:T(8,128)(2,1)} %copy-done, bf16[4,2,8,1792]{3,2,1,0:T(8,128)(2,1)S(1)} %join.1.refs_0_, ...), custom_call_target="tpu_custom_call" | custom-call | tf_op jit(solution)/shard_map/update/pallas_call | solution.py:362
  (21 shorter events, 2.8 us)
Async XLA Ops:
  0.6 0.8 copy-start.1
  1.5 0.7 copy-start.2
  2.2 0.7 copy-start.3
  2.9 0.7 copy-start.4
  3.5 0.7 copy-start.5
  13.1 1.3 %copy-start = (bf16[2,256,1792]{2,1,0:T(8,128)(2,1)}, bf16[2,256,1792]{2,1,0:T(8,128)(2,1)S(1)}, u32[]{:S(2)}) copy-start(bf16[2,256,1792]{2,1,0:T(8,128)(2,1)S(1)} %get-tuple-element.12.proj) | copy-start | bytes 5505028
  14.4 24.5 %all-to-all-start = ((bf16[64,8,640]{2,1,0:T(8,128)(2,1)}), bf16[64,8,640]{2,1,0:T(8,128)(2,1)S(1)}, u32[]{:S(2)}, u32[]{:S(2)}) async-start(bf16[64,8,640]{2,1,0:T(8,128)(2,1)} %get-tuple-element.8), calls=%async_computation | async-start | bytes 1310720 | tf_op jit(solution)/shard_map/all_to_all | solution.py:324
  25.4 27.4 %collective-permute-start.3 = (bf16[2,8,1792]{2,1,0:T(8,128)(2,1)S(1)}, bf16[2,8,1792]{2,1,0:T(8,128)(2,1)S(1)}, u32[]{:S(2)}, u32[]{:S(2)}) collective-permute-start(bf16[2,8,1792]{2,1,0:T(8,128)(2,1)S(1)} %get-tuple-element.11.refs_0_), channel_id=1, source_target_pairs={{0,384},{16,400},{32,416},{48,432},{64,448},{80,464},{96,480},{112... | collective-permute-start | bytes 172040 | tf_op jit(solution)/shard_map/ppermute | solution.py:325
  30.9 21.9 %collective-permute-start.2 = (bf16[2,8,1792]{2,1,0:T(8,128)(2,1)S(1)}, bf16[2,8,1792]{2,1,0:T(8,128)(2,1)S(1)}, u32[]{:S(2)}, u32[]{:S(2)}) collective-permute-start(bf16[2,8,1792]{2,1,0:T(8,128)(2,1)S(1)} %get-tuple-element.11.refs_0_), channel_id=1, source_target_pairs={{0,256},{16,272},{32,288},{48,304},{64,320},{80,336},{96,352},{112... | collective-permute-start | bytes 172040 | tf_op jit(solution)/shard_map/ppermute | solution.py:325
  32.8 20.0 %collective-permute-start.1 = (bf16[2,8,1792]{2,1,0:T(8,128)(2,1)S(1)}, bf16[2,8,1792]{2,1,0:T(8,128)(2,1)S(1)}, u32[]{:S(2)}, u32[]{:S(2)}) collective-permute-start(bf16[2,8,1792]{2,1,0:T(8,128)(2,1)S(1)} %get-tuple-element.11.refs_0_), channel_id=1, source_target_pairs={{0,128},{16,144},{32,160},{48,176},{64,192},{80,208},{96,224},{112... | collective-permute-start | bytes 172040 | tf_op jit(solution)/shard_map/ppermute | solution.py:325
  39.6 33.0 %all-to-all-start.1 = ((bf16[8,8,512]{2,1,0:T(8,128)(2,1)}), bf16[8,8,512]{2,1,0:T(8,128)(2,1)S(1)}, u32[]{:S(2)}, u32[]{:S(2)}) async-start(bf16[8,8,512]{2,1,0:T(8,128)(2,1)} %get-tuple-element.9), calls=%async_computation.1 | async-start | bytes 131072 | tf_op jit(solution)/shard_map/all_to_all | solution.py:337
  52.9 19.7 %collective-permute-start.6 = (bf16[4,2,8,1792]{3,2,1,0:T(8,128)(2,1)S(1)}, bf16[4,2,8,1792]{3,2,1,0:T(8,128)(2,1)S(1)}, u32[]{:S(2)}, u32[]{:S(2)}) collective-permute-start(bf16[4,2,8,1792]{3,2,1,0:T(8,128)(2,1)S(1)} %join.1.refs_0_), channel_id=1, source_target_pairs={{0,96},{16,112},{32,64},{48,80},{64,32},{80,48},{96,0},{112,16},{1... | collective-permute-start | bytes 688136 | tf_op jit(solution)/shard_map/ppermute | solution.py:347
  55.5 17.0 %collective-permute-start.5 = (bf16[4,2,8,1792]{3,2,1,0:T(8,128)(2,1)S(1)}, bf16[4,2,8,1792]{3,2,1,0:T(8,128)(2,1)S(1)}, u32[]{:S(2)}, u32[]{:S(2)}) collective-permute-start(bf16[4,2,8,1792]{3,2,1,0:T(8,128)(2,1)S(1)} %join.1.refs_0_), channel_id=1, source_target_pairs={{0,64},{16,80},{32,96},{48,112},{64,0},{80,16},{96,32},{112,48},{1... | collective-permute-start | bytes 688136 | tf_op jit(solution)/shard_map/ppermute | solution.py:347
  58.7 13.9 %collective-permute-start.4 = (bf16[4,2,8,1792]{3,2,1,0:T(8,128)(2,1)S(1)}, bf16[4,2,8,1792]{3,2,1,0:T(8,128)(2,1)S(1)}, u32[]{:S(2)}, u32[]{:S(2)}) collective-permute-start(bf16[4,2,8,1792]{3,2,1,0:T(8,128)(2,1)S(1)} %join.1.refs_0_), channel_id=1, source_target_pairs={{0,32},{16,48},{32,0},{48,16},{64,96},{80,112},{96,64},{112,80},{1... | collective-permute-start | bytes 688136 | tf_op jit(solution)/shard_map/ppermute | solution.py:347
  61.9 10.7 %collective-permute-start = (bf16[2,128,256]{2,1,0:T(8,128)(2,1)S(1)}, bf16[2,128,256]{2,1,0:T(8,128)(2,1)S(1)}, u32[]{:S(2)}, u32[]{:S(2)}) collective-permute-start(bf16[2,128,256]{2,1,0:T(8,128)(2,1)S(1)} %get-tuple-element.10.refs_4_.near), channel_id=1, source_target_pairs={{0,256},{16,272},{32,288},{48,304},{64,320},{80,336},{96,352},{112... | collective-permute-start | bytes 393224 | tf_op jit(solution)/shard_map/ppermute | solution.py:338
  74.0 15.9 %all-to-all-start.2 = ((bf16[64,8,384]{2,1,0:T(8,128)(2,1)}), bf16[64,8,384]{2,1,0:T(8,128)(2,1)S(1)}, u32[]{:S(2)}, u32[]{:S(2)}) async-start(bf16[64,8,384]{2,1,0:T(8,128)(2,1)} %moment.1), calls=%async_computation.2 | async-start | bytes 786432 | tf_op jit(solution)/shard_map/all_to_all | solution.py:356
  78.8 8.8 %collective-permute-start.7 = (bf16[4,2,8,1792]{3,2,1,0:T(8,128)(2,1)S(1)}, bf16[4,2,8,1792]{3,2,1,0:T(8,128)(2,1)S(1)}, u32[]{:S(2)}, u32[]{:S(2)}) collective-permute-start(bf16[4,2,8,1792]{3,2,1,0:T(8,128)(2,1)S(1)} %join.1.refs_0_), channel_id=1, source_target_pairs={{0,16},{16,0},{32,48},{48,32},{64,80},{80,64},{96,112},{112,96},{1... | collective-permute-start | bytes 688136 | tf_op jit(solution)/shard_map/ppermute | solution.py:357
  81.3 6.3 %collective-permute-start.10 = (bf16[4,2,8,1792]{3,2,1,0:T(8,128)(2,1)S(1)}, bf16[4,2,8,1792]{3,2,1,0:T(8,128)(2,1)S(1)}, u32[]{:S(2)}, u32[]{:S(2)}) collective-permute-start(bf16[4,2,8,1792]{3,2,1,0:T(8,128)(2,1)S(1)} %collective-permute-done.6.refs_2_.refs_3_), channel_id=1, source_target_pairs={{0,16},{16,0},{32,48},{48,32},{64,80},{80,64},{96,112},{112,96},{1... | collective-permute-start | bytes 688136 | tf_op jit(solution)/shard_map/ppermute | solution.py:357
  83.3 4.4 %collective-permute-start.9 = (bf16[4,2,8,1792]{3,2,1,0:T(8,128)(2,1)S(1)}, bf16[4,2,8,1792]{3,2,1,0:T(8,128)(2,1)S(1)}, u32[]{:S(2)}, u32[]{:S(2)}) collective-permute-start(bf16[4,2,8,1792]{3,2,1,0:T(8,128)(2,1)S(1)} %collective-permute-done.5.refs_1_.refs_2_), channel_id=1, source_target_pairs={{0,16},{16,0},{32,48},{48,32},{64,80},{80,64},{96,112},{112,96},{1... | collective-permute-start | bytes 688136 | tf_op jit(solution)/shard_map/ppermute | solution.py:357
  85.7 3.4 %collective-permute-start.8 = (bf16[4,2,8,1792]{3,2,1,0:T(8,128)(2,1)S(1)}, bf16[4,2,8,1792]{3,2,1,0:T(8,128)(2,1)S(1)}, u32[]{:S(2)}, u32[]{:S(2)}) collective-permute-start(bf16[4,2,8,1792]{3,2,1,0:T(8,128)(2,1)S(1)} %collective-permute-done.4.refs_0_.refs_1_), channel_id=1, source_target_pairs={{0,16},{16,0},{32,48},{48,32},{64,80},{80,64},{96,112},{112,96},{1... | collective-permute-start | bytes 688136 | tf_op jit(solution)/shard_map/ppermute | solution.py:357
